TPU v7x, 256 devices: a whole 4x4x8 slice. The times are simulated.
256 devices in a mesh: dom: 64 (over z, y, core), rel: 4 (over x).
Axes of the slice: x: 4, y: 4, z: 8, core: 2. Of those that a mesh axis runs over, the one named last changes fastest.
Arguments:
- embeddings: float32 [131072, 400], P('dom'), may hold values from -3 to 3
- rel_weight: float32 [256, 400], P('rel'), may hold values from -4 to 4
- head_row: int32 [98304], P(('dom', 'rel')), may hold values from 0 to 2047
- rel_id: int32 [98304], P(('dom', 'rel')), may hold values from 0 to 63
- tail_owner: int32 [98304, 1], P(('dom', 'rel')), may hold values from 0 to 63; in each aligned block of 384 rows (0 to 383, 384 to 767, ...) at most 12 rows name the same one
- tail_row: int32 [98304], P(('dom', 'rel')), may hold values from 0 to 2047
- neg_owner: int32 [24576, 1], P('dom'), may hold values from 0 to 63; in each aligned block of 96 rows (0 to 95, 96 to 191, ...) at most 3 rows name the same one
- neg_row: int32 [24576], P('dom'), may hold values from 0 to 2047
Outputs:
- embedding_grad: float32 [131072, 400], P('dom')
- relation_grad: float32 [256, 400], P('rel')
Inputs may be any that keep to these rules, and one draw needn't show every extreme that they name: `tail_owner`: in the rows of one device no partition is named more than 12 times, and it is reached. `neg_owner`: in each aligned block of 96 rows no partition is named more than 3 times, and it is reached.
All inputs are finite; a program needn't handle non-finite values.
Results may differ from a plain program's by a relative error of at most 0.0003.
Values sent between devices are 32-bit elements; how exact they have to be, the bound alone decides.
A program may use at most 64 MiB of HBM per device.

v0:
```python
import jax
import jax.numpy as jnp
from jax import lax
from jax.sharding import PartitionSpec as P

SPAN = 128
NEG = 128


def span_grads(head_emb, rel_rows, tail_emb, neg_emb):
    queries = head_emb * rel_rows
    positive = jnp.sum(queries * tail_emb, axis=1)
    scores = jnp.dot(queries, neg_emb.T, precision=lax.Precision.HIGHEST)
    row_max = jnp.maximum(positive, jnp.max(scores, axis=1))
    pos_exp = jnp.exp(positive - row_max)
    neg_exp = jnp.exp(scores - row_max[:, None])
    total = pos_exp + jnp.sum(neg_exp, axis=1)
    pos_coef = pos_exp / total - 1.0
    neg_coef = neg_exp / total[:, None]
    grad_query = pos_coef[:, None] * tail_emb + jnp.dot(
        neg_coef, neg_emb, precision=lax.Precision.HIGHEST
    )
    grad_tail = pos_coef[:, None] * queries
    grad_neg = jnp.dot(neg_coef.T, queries, precision=lax.Precision.HIGHEST)
    return (grad_query * rel_rows, grad_query * head_emb, grad_tail, grad_neg)


def slot_of(owner, dom_count, capacity):
    onehot = (owner[:, None] == jnp.arange(dom_count, dtype=jnp.int32)[None, :]).astype(jnp.int32)
    position = jnp.sum((jnp.cumsum(onehot, axis=0) - 1) * onehot, axis=1)
    return owner * capacity + position


def id_buffer(slot_index, rows, dom_count, capacity):
    filled = jnp.zeros((dom_count * capacity,), jnp.int32).at[slot_index].set(rows)
    return filled.reshape(dom_count, capacity)


def grad_buffer(slot_index, values, dom_count, capacity):
    filled = (
        jnp.zeros((dom_count * capacity, values.shape[1]), jnp.float32).at[slot_index].set(values)
    )
    return filled.reshape(dom_count, capacity, values.shape[1])


def serve(embeddings, asked):
    width = embeddings.shape[1]
    return embeddings[asked.reshape(-1)].reshape(asked.shape[0], asked.shape[1], width)


def body(embeddings, rel_weight, head_row, rel_id, tail_owner, tail_row, neg_owner, neg_row):
    dom_count = lax.axis_size("dom")
    rel_count = lax.axis_size("rel")
    width = embeddings.shape[1]
    edges = head_row.shape[0]
    neg_total = neg_row.shape[0]
    spans = edges // SPAN
    part_len = neg_total // rel_count
    tail_cap = 2 * edges // dom_count
    part_cap = 2 * part_len // dom_count
    tail_slot = slot_of(tail_owner[:, 0], dom_count, tail_cap)
    tail_ids = id_buffer(tail_slot, tail_row, dom_count, tail_cap)
    neg_cap = rel_count * part_cap
    neg_slot = slot_of(neg_owner[:, 0], dom_count, neg_cap)
    neg_ids = id_buffer(neg_slot, neg_row, dom_count, neg_cap)
    asked_tail, asked_neg = (
        lax.all_to_all(tail_ids, "dom", split_axis=0, concat_axis=0, tiled=True),
        lax.all_to_all(neg_ids, "dom", split_axis=0, concat_axis=0, tiled=True),
    )
    got_tail, got_neg = (
        lax.all_to_all(
            serve(embeddings, asked_tail), "dom", split_axis=0, concat_axis=0, tiled=True
        ),
        lax.all_to_all(
            serve(embeddings, asked_neg), "dom", split_axis=0, concat_axis=0, tiled=True
        ),
    )
    neg_emb = got_neg.reshape(-1, width)[neg_slot]
    tail_emb = got_tail.reshape(-1, width)[tail_slot]
    head_emb = embeddings[head_row]
    rel_rows = rel_weight[rel_id]
    grad_head, grad_rel, grad_tail, grad_neg = jax.vmap(span_grads)(
        head_emb.reshape(spans, SPAN, width),
        rel_rows.reshape(spans, SPAN, width),
        tail_emb.reshape(spans, SPAN, width),
        neg_emb.reshape(spans, NEG, width),
    )
    slab_grad = (
        jnp.zeros(embeddings.shape, jnp.float32).at[head_row].add(grad_head.reshape(-1, width))
    )
    rel_local = jnp.zeros(rel_weight.shape, jnp.float32).at[rel_id].add(grad_rel.reshape(-1, width))
    tail_back = grad_buffer(tail_slot, grad_tail.reshape(-1, width), dom_count, tail_cap)
    neg_back = grad_buffer(neg_slot, grad_neg.reshape(-1, width), dom_count, rel_count * part_cap)
    recv_tail, recv_neg = (
        lax.all_to_all(tail_back, "dom", split_axis=0, concat_axis=0, tiled=True),
        lax.all_to_all(neg_back, "dom", split_axis=0, concat_axis=0, tiled=True),
    )
    slab_grad = slab_grad.at[asked_tail.reshape(-1)].add(recv_tail.reshape(-1, width))
    slab_grad = slab_grad.at[asked_neg.reshape(-1)].add(recv_neg.reshape(-1, width))
    embedding_grad = lax.psum(slab_grad, "rel")
    relation_grad = lax.psum(rel_local, "dom")
    return (embedding_grad, relation_grad)


def solution(mesh):
    return jax.shard_map(
        body,
        mesh=mesh,
        in_specs=(
            P("dom", None),
            P("rel", None),
            P(("dom", "rel")),
            P(("dom", "rel")),
            P(("dom", "rel"), None),
            P(("dom", "rel")),
            P("dom", None),
            P("dom"),
        ),
        out_specs=(P("dom", None), P("rel", None)),
        check_vma=False,
    )
```

profile of v0, /device:TPU:2, one launch (start us, length us, event | category | flops | bytes accessed | tf_op | source)
XLA Modules:
  0.0 591.6 jit_solution(2802582018687139575)
XLA Ops:
  9.9 3.1 scatter_custom_fusion
  13.7 12.1 %all-to-all-start = ((s32[64,1,12]{2,1,0:T(1,128)}), s32[64,1,12]{2,1,0:T(1,128)S(1)}, u32[]{:S(2)}, u32[]{:S(2)}) async-start(s32[64,1,12]{2,1,0:T(1,128)} %bitcast.1), calls=%async_computation | async-start | bytes 65536 | tf_op jit(solution)/shard_map/all_to_all | solution.py:67
  28.5 5.0 copy.41
  33.5 3.1 scatter_custom_fusion.1
  37.3 10.3 %all-to-all-start.2 = ((s32[64,1,12]{2,1,0:T(1,128)}), s32[64,1,12]{2,1,0:T(1,128)S(1)}, u32[]{:S(2)}, u32[]{:S(2)}) async-start(s32[64,1,12]{2,1,0:T(1,128)} %bitcast.6), calls=%async_computation.2 | async-start | bytes 65536 | tf_op jit(solution)/shard_map/all_to_all | solution.py:68
  49.0 5.0 gather_fusion.2
  57.2 8.7 %all-to-all-start.1 = ((f32[64,12,400]{2,1,0:T(8,128)}), f32[64,12,400]{2,1,0:T(8,128)S(1)}, u32[]{:S(2)}, u32[]{:S(2)}) async-start(f32[64,12,400]{2,1,0:T(8,128)} %reshape.203), calls=%async_computation.1 | async-start | bytes 4194304 | tf_op jit(solution)/shard_map/all_to_all | solution.py:71
  66.7 5.7 gather_fusion.4
  75.1 42.2 %all-to-all-done.1 = f32[64,12,400]{2,1,0:T(8,128)S(1)} async-done(((f32[64,12,400]{2,1,0:T(8,128)}), f32[64,12,400]{2,1,0:T(8,128)S(1)}, u32[]{:S(2)}, u32[]{:S(2)}) %all-to-all-start.1) | async-done | bytes 1228832 | tf_op jit(solution)/shard_map/all_to_all | solution.py:71
  118.6 6.1 %all-to-all-start.3 = ((f32[64,12,400]{2,1,0:T(8,128)}), f32[64,12,400]{2,1,0:T(8,128)}, u32[]{:S(2)}, u32[]{:S(2)}) async-start(f32[64,12,400]{2,1,0:T(8,128)} %reshape.209), calls=%async_computation.3 | async-start | bytes 4194304 | tf_op jit(solution)/shard_map/all_to_all | solution.py:74
  124.7 4.2 gather_fusion
  138.7 37.1 %all-to-all-done.3 = f32[64,12,400]{2,1,0:T(8,128)} async-done(((f32[64,12,400]{2,1,0:T(8,128)}), f32[64,12,400]{2,1,0:T(8,128)}, u32[]{:S(2)}, u32[]{:S(2)}) %all-to-all-start.3) | async-done | bytes 1228832 | tf_op jit(solution)/shard_map/all_to_all | solution.py:74
  186.5 5.7 all-to-all-start.4
  198.4 45.0 %all-to-all-done.4 = f32[64,12,400]{2,1,0:T(8,128)} async-done(((f32[64,12,400]{2,1,0:T(8,128)}), f32[64,12,400]{2,1,0:T(8,128)}, u32[]{:S(2)}, u32[]{:S(2)}) %all-to-all-start.4) | async-done | bytes 1228832 | tf_op jit(solution)/shard_map/all_to_all | solution.py:95
  243.4 5.6 all-to-all-start.5
  251.7 3.3 fusion.36
  256.4 5.0 scatter_custom_fusion.2
  263.0 10.7 %scatter_fusion = f32[2048,400]{1,0:T(8,128)} fusion(f32[2048,400]{1,0:T(8,128)} %scatter_custom_fusion.2, s32[768]{0:T(1024)S(1)} %fusion.24, f32[768,400]{1,0:T(8,128)S(1)} %reshape.304), kind=kCustom, calls=%fused_computation.10 | custom fusion | flops 307200 | bytes 3689472 | tf_op jit(solution)/shard_map/scatter-add | solution.py:98
  273.7 26.5 %all-to-all-done.5 = f32[64,12,400]{2,1,0:T(8,128)} async-done(((f32[64,12,400]{2,1,0:T(8,128)}), f32[64,12,400]{2,1,0:T(8,128)}, u32[]{:S(2)}, u32[]{:S(2)}) %all-to-all-start.5) | async-done | bytes 1228832 | tf_op jit(solution)/shard_map/all_to_all | solution.py:96
  301.8 10.7 %scatter_fusion.1 = f32[2048,400]{1,0:T(8,128)} fusion(f32[2048,400]{1,0:T(8,128)} %scatter_fusion, s32[768]{0:T(1024)S(1)} %fusion.25, f32[768,400]{1,0:T(8,128)S(1)} %reshape.320), kind=kCustom, calls=%fused_computation.12 | custom fusion | flops 307200 | bytes 3689472 | tf_op jit(solution)/shard_map/scatter-add | solution.py:99
  313.1 3.4 scatter_custom_fusion.7
  316.6 89.1 %all-reduce.3.cloned.1.call-done = f32[2048,400]{1,0:T(8,128)} async-done(((f32[2048,400]{1,0:T(8,128)}), f32[2048,400]{1,0:T(8,128)}) %all-reduce.3.cloned.1.call-update) | async-done | bytes 3276816 | tf_op jit(solution)/shard_map/psum | solution.py:100
  405.7 5.2 copy.66
  410.9 172.1 %all-reduce.5.cloned.1.call-done = f32[64,400]{1,0:T(8,128)} async-done(((f32[64,400]{1,0:T(8,128)}), f32[64,400]{1,0:T(8,128)}) %all-reduce.5.cloned.1.call-update) | async-done | bytes 102416 | tf_op jit(solution)/shard_map/psum | solution.py:101
  (82 shorter events, 52.2 us)
Async XLA Ops:
  7.2 122.4 %copy-start = (f32[64,400]{1,0:T(8,128)S(1)}, f32[64,400]{1,0:T(8,128)}, u32[]{:S(2)}) copy-start(f32[64,400]{1,0:T(8,128)} %param.9) | copy-start | bytes 307204
  13.7 23.6 %all-to-all-start = ((s32[64,1,12]{2,1,0:T(1,128)}), s32[64,1,12]{2,1,0:T(1,128)S(1)}, u32[]{:S(2)}, u32[]{:S(2)}) async-start(s32[64,1,12]{2,1,0:T(1,128)} %bitcast.1), calls=%async_computation | async-start | bytes 65536 | tf_op jit(solution)/shard_map/all_to_all | solution.py:67
  37.3 19.8 %all-to-all-start.2 = ((s32[64,1,12]{2,1,0:T(1,128)}), s32[64,1,12]{2,1,0:T(1,128)S(1)}, u32[]{:S(2)}, u32[]{:S(2)}) async-start(s32[64,1,12]{2,1,0:T(1,128)} %bitcast.6), calls=%async_computation.2 | async-start | bytes 65536 | tf_op jit(solution)/shard_map/all_to_all | solution.py:68
  57.2 60.0 %all-to-all-start.1 = ((f32[64,12,400]{2,1,0:T(8,128)}), f32[64,12,400]{2,1,0:T(8,128)S(1)}, u32[]{:S(2)}, u32[]{:S(2)}) async-start(f32[64,12,400]{2,1,0:T(8,128)} %reshape.203), calls=%async_computation.1 | async-start | bytes 4194304 | tf_op jit(solution)/shard_map/all_to_all | solution.py:71
  75.1 49.6 %copy-start.6 = (s32[384]{0:T(512)S(1)}, s32[384]{0:T(512)}, u32[]{:S(2)}) copy-start(s32[384]{0:T(512)} %param.10) | copy-start | bytes 4612
  117.2 1.3 copy-start.1
  118.6 57.3 %all-to-all-start.3 = ((f32[64,12,400]{2,1,0:T(8,128)}), f32[64,12,400]{2,1,0:T(8,128)}, u32[]{:S(2)}, u32[]{:S(2)}) async-start(f32[64,12,400]{2,1,0:T(8,128)} %reshape.209), calls=%async_computation.3 | async-start | bytes 4194304 | tf_op jit(solution)/shard_map/all_to_all | solution.py:74
  128.9 0.7 copy-start.7
  186.5 5.8 copy-start.4
  186.5 56.9 %all-to-all-start.4 = ((f32[64,12,400]{2,1,0:T(8,128)}), f32[64,12,400]{2,1,0:T(8,128)}, u32[]{:S(2)}, u32[]{:S(2)}) async-start(f32[64,12,400]{2,1,0:T(8,128)} %reshape.214), calls=%async_computation.4 | async-start | bytes 4194304 | tf_op jit(solution)/shard_map/all_to_all | solution.py:95
  243.4 56.8 %all-to-all-start.5 = ((f32[64,12,400]{2,1,0:T(8,128)}), f32[64,12,400]{2,1,0:T(8,128)}, u32[]{:S(2)}, u32[]{:S(2)}) async-start(f32[64,12,400]{2,1,0:T(8,128)} %reshape.217), calls=%async_computation.5 | async-start | bytes 4194304 | tf_op jit(solution)/shard_map/all_to_all | solution.py:96
  249.0 1.6 copy-start.3
  249.0 156.7 %all-reduce.3.cloned.1.call-start = ((), (), s32[]{:S(2)}) async-start(), calls=%async_computation.6 | async-start | bytes 8388608 | tf_op jit(solution)/shard_map/psum | solution.py:100
  249.5 2.2 copy-start.2
  250.6 1.1 copy-start.5
  312.6 270.4 %all-reduce.5.cloned.1.call-start = ((), (), s32[]{:S(2)}) async-start(), calls=%async_computation.7 | async-start | bytes 262144 | tf_op jit(solution)/shard_map/psum | solution.py:101
Sparse Core Ops, SparseCore 0:
  312.7 92.9 all-reduce.2
  410.1 172.8 all-reduce.4
where the time goes:
time: 603 us; the launch traced here: 592 us
  waiting for transfers between devices  414 us (69%)
  local copies, waits for them, and re-layouts  64.5 us (11%)
  starting transfers between devices  48.9 us (8%)
  other arithmetic  42.6 us (7%)
  between operations  14.6 us (2%)
  matrix products  7.26 us (1%)
    psum x1, waiting for transfers between devices, body(): relation_grad = lax.psum(rel_local, 'dom')  172 us
    psum x1, waiting for transfers between devices, body(): embedding_grad = lax.psum(slab_grad, 'rel')  89.1 us
    all_to_all x1, waiting for transfers between devices, body(): lax.all_to_all(tail_back, 'dom', split_axis=0, concat_axis=0, tiled=True)  45 us
    all_to_all x1, waiting for transfers between devices, body(): lax.all_to_all(serve(embeddings, asked_tail), 'dom', split_axis=0, concat...  42.2 us
    all_to_all x1, waiting for transfers between devices, body(): lax.all_to_all(serve(embeddings, asked_neg), 'dom', split_axis=0, concat_...  37.1 us
    all_to_all x1, waiting for transfers between devices, body(): lax.all_to_all(neg_back, 'dom', split_axis=0, concat_axis=0, tiled=True)  26.5 us
    unnamed x19, local copies, waits for them, and re-layouts  13.4 us
    all_to_all x1, starting transfers between devices, body(): lax.all_to_all(tail_ids, 'dom', split_axis=0, concat_axis=0, tiled=True)  12.1 us
  transfers between devices with their start and end apart: 8, of which 7 were waited for; matrix products, arithmetic and copies ran while one was open for 14% of the time, Pallas kernels for 0%

commit v1 on v0

v1 whole, which is shorter than its diff:
```python
import functools

import jax
import jax.numpy as jnp
from jax import lax
from jax.experimental import pallas as pl
from jax.experimental.pallas import tpu as pltpu
from jax.sharding import PartitionSpec as P

SPAN = 128
MAIN = 384
WIDE = 512
SLOTS = 16
CAP_T = 12
F32, BF16, I32 = jnp.float32, jnp.bfloat16, jnp.int32
MESH = pl.DeviceIdType.MESH
HIGHEST = lax.Precision.HIGHEST
NN = (((1,), (0,)), ((), ()))
NT = (((1,), (1,)), ((), ()))
TN = (((0,), (0,)), ((), ()))


def iota(shape, dim):
    return lax.broadcasted_iota(I32, shape, dim)


def parts(x, count):
    out = []
    for _ in range(count - 1):
        hi = x.astype(BF16)
        out.append(hi)
        x = x - hi.astype(F32)
    return out + [x.astype(BF16)]


def dot(a, b, dims):
    return lax.dot_general(a, b, dims, preferred_element_type=F32)


def dot_parts(onehot, values, dims=NN):
    total = dot(onehot, values[0], dims)
    for v in values[1:]:
        total = total + dot(onehot, v, dims)
    return total


def column(row):
    n = row.shape[1]
    return jnp.broadcast_to(row.astype(F32), (8, n)).T[:, 0:1].astype(I32)


def onehot(mask):
    return jnp.where(mask, 1.0, 0.0).astype(BF16)


def fold_matrix(rows, cols):
    l, m = iota((rows, cols), 0), iota((rows, cols), 1)
    return onehot((l & 15) == m)


def spread_matrix(rows, cols):
    m, l = iota((rows, cols), 0), iota((rows, cols), 1)
    return onehot((l & 15) == m)


def route_kernel(owner_ref, row_ref, ids_ref, slot_ref):
    lists = owner_ref.shape[1]
    owner = owner_ref[...]
    same = column(owner) == owner
    earlier = iota((lists, lists), 0) < iota((lists, lists), 1)
    position = jnp.sum(jnp.where(same & earlier, 1, 0), axis=0, keepdims=True)
    negative = owner >= 64
    valid = owner < 128
    position = jnp.where(negative, position + CAP_T, position)
    owner = jnp.where(negative, owner - 64, owner)
    slot_ref[...] = jnp.where(valid, owner * SLOTS + position, -1)
    peers = ids_ref.shape[0]
    left = jnp.where((iota((peers, lists), 0) == owner) & valid, (row_ref[...] + 1).astype(F32), 0.0)
    right = jnp.where(iota((128, lists), 0) == position, 1.0, 0.0)
    ids = lax.dot_general(left, right, NT, precision=HIGHEST, preferred_element_type=F32)
    ids_ref[...] = (ids + 0.5).astype(I32) - 1


def id_column(ids):
    p = ids.shape[0]
    spread = jnp.broadcast_to(ids.astype(F32)[:, None, :], (p, SLOTS, 128))
    own = iota((p, SLOTS, 128), 1) == iota((p, SLOTS, 128), 2)
    return jnp.sum(jnp.where(own, spread, 0.0), axis=2, keepdims=True).reshape(p * SLOTS, 1).astype(I32)


def split_table(et_ref, tables, copies):
    width, rows = et_ref.shape

    @pl.loop(0, width // 16)
    def _(i):
        at = pl.multiple_of(i * 16, 16)
        for t, v in zip(tables, parts(et_ref[pl.ds(at, 16), :], 3), strict=True):
            t[pl.ds(at, 16), :] = v

    for t in tables:
        tail = t[MAIN : MAIN + 16, :]
        for k in range(1, 8):
            t[MAIN + 16 * k : MAIN + 16 * (k + 1), :] = tail if copies else jnp.zeros_like(tail)


def serve_kernel(ids_ref, et_ref, out_ref, hi_ref, mid_ref, lo_ref):
    tables = (hi_ref, mid_ref, lo_ref)
    split_table(et_ref, tables, True)
    rows = et_ref.shape[1]
    group = 16

    @pl.loop(0, ids_ref.shape[0] // group)
    def _(i):
        at = pl.multiple_of(i * group, group)
        ids = id_column(ids_ref[pl.ds(at, group), :])
        hot = onehot(iota((group * SLOTS, rows), 1) == ids)
        got = dot_parts(hot, [t[...] for t in tables], NT)
        slot = iota((group, SLOTS, 128), 1)
        lane = iota((group, SLOTS, 128), 2)
        rest = got[:, MAIN:].reshape(group, SLOTS, 128)
        rest = jnp.where((lane >> 4) == (slot & 7), rest, 0.0)
        low = jnp.sum(jnp.where(slot < 8, rest, 0.0), axis=1, keepdims=True)
        high = jnp.sum(jnp.where(slot < 8, 0.0, rest), axis=1, keepdims=True)
        for k, part in enumerate((low, high, jnp.zeros_like(low))):
            main = got[:, 128 * k : 128 * (k + 1)].reshape(group, SLOTS, 128)
            out_ref[pl.ds(at, group), :, 128 * k : 128 * (k + 1)] = jnp.where(slot == SLOTS - 1, part, main)


def heads_kernel(head_ref, rel_id_ref, et_ref, rel_ref, head_out, rel_out, hi_ref, mid_ref, lo_ref):
    tables = (hi_ref, mid_ref, lo_ref)
    split_table(et_ref, tables, False)
    edges, rows = head_ref.shape[1], et_ref.shape[1]
    hot = onehot(iota((edges, rows), 1) == column(head_ref[...]))
    head_out[...] = dot_parts(hot, [t[...] for t in tables], NT)
    groups, width = rel_ref.shape
    hot_rel = onehot(iota((edges, groups), 1) == column(rel_id_ref[...]))
    got = dot_parts(hot_rel, parts(rel_ref[...], 3))
    rel_out[...] = jnp.concatenate([got, jnp.zeros((edges, WIDE - width), F32)], axis=1)


def unpack_kernel(slot_ref, recv_ref, out_ref, neg_ref):
    lists = slot_ref.shape[1]
    peers = recv_ref.shape[0]
    slot = column(slot_ref[...])
    hot = onehot(iota((lists, peers * SLOTS), 1) == slot)
    main = dot_parts(hot, parts(recv_ref[...].reshape(peers * SLOTS, MAIN), 3))
    hot_peer = onehot(iota((lists, peers), 1) == (slot >> 4))
    rest = dot_parts(hot_peer, parts(recv_ref[:, SLOTS - 1, 0:256], 3))
    rest = jnp.where((iota((lists, 256), 1) >> 4) == (slot & 15), rest, 0.0)
    fold = fold_matrix(256, 128)
    rest = sum(dot(p, fold, NN) for p in parts(rest, 3))
    out_ref[:, 0:MAIN] = main[0 : out_ref.shape[0]]
    out_ref[:, MAIN:WIDE] = rest[0 : out_ref.shape[0]]
    first, count = out_ref.shape[0], neg_ref.shape[0]
    neg_ref[:, 0:MAIN] = main[first : first + count]
    neg_ref[:, MAIN:WIDE] = rest[first : first + count]


def grads_kernel(head_ref, relrow_ref, tail_ref, neg_ref, rel_id_ref, gh_ref, gt_ref, gn_ref, gr_ref):
    edges = head_ref.shape[0]
    groups = gr_ref.shape[0]
    for c in range(edges // SPAN):
        at = slice(c * SPAN, (c + 1) * SPAN)
        head, rel, tail, neg = head_ref[at], relrow_ref[at], tail_ref[at], neg_ref[at]
        queries = head * rel
        positive = jnp.sum(queries * tail, axis=1, keepdims=True)
        scores = lax.dot_general(queries, neg, NT, precision=HIGHEST, preferred_element_type=F32)
        row_max = jnp.maximum(positive, jnp.max(scores, axis=1, keepdims=True))
        pos_exp = jnp.exp(positive - row_max)
        neg_exp = jnp.exp(scores - row_max)
        total = pos_exp + jnp.sum(neg_exp, axis=1, keepdims=True)
        pos_coef = pos_exp / total - 1.0
        neg_coef = neg_exp / total
        grad_query = pos_coef * tail + lax.dot_general(neg_coef, neg, NN, precision=HIGHEST, preferred_element_type=F32)
        gh_ref[at] = grad_query * rel
        gt_ref[at] = pos_coef * queries
        gn_ref[at] = lax.dot_general(neg_coef.T, queries, NN, precision=HIGHEST, preferred_element_type=F32)
        hot = onehot(iota((groups, SPAN), 0) == rel_id_ref[:, at])
        part = dot_parts(hot, parts(grad_query * head, 3))
        if c == 0:
            gr_ref[...] = part
        else:
            gr_ref[...] += part


def pack_kernel(slot_ref, gt_ref, gn_ref, out_ref):
    lists = slot_ref.shape[1]
    peers = out_ref.shape[0]
    edges, quarter = gt_ref.shape[0], gn_ref.shape[0]
    slot = slot_ref[...]
    values = jnp.concatenate([gt_ref[...], gn_ref[...], jnp.zeros((lists - edges - quarter, WIDE), F32)], axis=0)
    hot = onehot(iota((peers * SLOTS, lists), 0) == slot)
    main = dot_parts(hot, parts(values[:, 0:MAIN], 3)).reshape(peers, SLOTS, MAIN)
    spread = spread_matrix(128, 256)
    rest = sum(dot(p, spread, NN) for p in parts(values[:, MAIN:WIDE], 3))
    rest = jnp.where((iota((lists, 256), 1) >> 4) == (column(slot) & 15), rest, 0.0)
    hot_peer = onehot(iota((peers, lists), 0) == (slot >> 4))
    rest = dot_parts(hot_peer, parts(rest, 3))
    rest = jnp.concatenate([rest, jnp.zeros((peers, MAIN - 256), F32)], axis=1)
    last = iota((peers, SLOTS, MAIN), 1) == SLOTS - 1
    out_ref[...] = jnp.where(last, rest[:, None, :], main)


def scatter_kernel(ids_ref, recv_ref, gh_ref, head_ref, out_ref, hi_ref, lo_ref):
    peers = recv_ref.shape[0]
    slots = peers * SLOTS
    edges = gh_ref.shape[0]
    width, rows = out_ref.shape
    for b in range(0, peers, 16):
        n = 16 * SLOTS
        rest = jnp.broadcast_to(recv_ref[b : b + 16, SLOTS - 1 : SLOTS, 0:256], (16, SLOTS, 256))
        mine = (iota((16, SLOTS, 256), 2) >> 4) == iota((16, SLOTS, 256), 1)
        rest = jnp.where(mine, rest, 0.0).reshape(n, 256)
        fold = fold_matrix(256, 128)
        rest = sum(dot(p, fold, NN) for p in parts(rest, 2))
        main = recv_ref[b : b + 16].reshape(n, MAIN)
        at = slice(b * SLOTS, (b + 16) * SLOTS)
        hi, lo = parts(main.T, 2)
        hi_ref[0:MAIN, at], lo_ref[0:MAIN, at] = hi, lo
        hi, lo = parts(rest.T, 2)
        hi_ref[MAIN:WIDE, at], lo_ref[MAIN:WIDE, at] = hi, lo
    hi, lo = parts(gh_ref[...].T, 2)
    hi_ref[:, slots:], lo_ref[:, slots:] = hi, lo
    ids = jnp.concatenate([id_column(ids_ref[...]), column(head_ref[...])], axis=0)
    step = 512

    @pl.loop(0, rows // step)
    def _(i):
        at = pl.multiple_of(i * step, step)
        hot = onehot(iota((slots + edges, step), 1) + at == ids)
        got = dot(hi_ref[...], hot, NN) + dot(lo_ref[...], hot, NN)
        out_ref[:, pl.ds(at, step)] = got[0:width]


def local_call(kernel, outs, scratch=(), vmem=48, flops=0, moved=0):
    single = not isinstance(outs, (list, tuple))
    return pl.pallas_call(
        kernel,
        out_shape=outs if single else tuple(outs),
        scratch_shapes=list(scratch),
        compiler_params=pltpu.CompilerParams(vmem_limit_bytes=vmem << 20),
        cost_estimate=pl.CostEstimate(flops=flops, bytes_accessed=moved, transcendentals=0),
        name=kernel.__name__.removesuffix("_kernel"),
    )


def shape(*dims, dtype=F32):
    return jax.ShapeDtypeStruct(dims, dtype)


def greet(n, me):
    barrier = pltpu.get_barrier_semaphore()
    for k in range(1, n):
        pl.semaphore_signal(barrier, inc=1, device_id={"rel": lax.rem(me + k, n)}, device_id_type=MESH)
    pl.semaphore_wait(barrier, n - 1)


def gather_kernel(n, in_ref, out_ref, send_sem, recv_sem, own_sem):
    me = lax.axis_index("rel")
    greet(n, me)
    copies = []
    for k in range(1, n):
        copy = pltpu.make_async_remote_copy(
            in_ref, out_ref.at[me], send_sem.at[k - 1], recv_sem.at[k - 1],
            device_id={"rel": lax.rem(me + k, n)}, device_id_type=MESH)
        copy.start()
        copies.append(copy)
    own = pltpu.make_async_copy(in_ref, out_ref.at[me], own_sem)
    own.start()
    own.wait()
    for copy in copies:
        copy.wait()


def reduce_kernel(n, in_ref, out_ref, held, send_sem, recv_sem):
    me = lax.axis_index("rel")
    greet(n, me)
    copies = []
    for k in range(1, n):
        peer = lax.rem(me + k, n)
        copy = pltpu.make_async_remote_copy(
            in_ref.at[peer], held.at[k - 1], send_sem.at[k - 1], recv_sem.at[k - 1],
            device_id={"rel": peer}, device_id_type=MESH)
        copy.start()
        copies.append(copy)
    for copy in copies:
        copy.wait()
    total = in_ref[me]
    for k in range(1, n):
        total = total + held[k - 1]
    out_ref[...] = total


def all_reduce_kernel(n, x_ref, out_ref, held, sums, send_sem, recv_sem):
    width, rows = x_ref.shape
    piece, half = rows // n, width // 2
    me = lax.axis_index("rel")
    right, left, far = lax.rem(me + 1, n), lax.rem(me + 3, n), lax.rem(me + 2, n)
    barrier = pltpu.get_barrier_semaphore()
    for peer in (right, left):
        pl.semaphore_signal(barrier, inc=1, device_id={"rel": peer}, device_id_type=MESH)
    pl.semaphore_wait(barrier, 2)

    def cols(j):
        return pl.ds(pl.multiple_of(j * piece, piece), piece)

    ways = ((right, left, slice(0, half), slice(half, width)), (left, right, slice(half, width), slice(0, half)))

    def send(way, slot, src, dst):
        copy = pltpu.make_async_remote_copy(
            src, dst, send_sem.at[way, slot], recv_sem.at[way, slot], device_id={"rel": ways[way][0]}, device_id_type=MESH)
        copy.start()
        return copy

    sent = {}
    for way, (to, _, mine, other) in enumerate(ways):
        sent[way, 0] = send(way, 0, x_ref.at[mine, cols(far)], held.at[way, 0])
        sent[way, 1] = send(way, 1, x_ref.at[other, cols(to)], held.at[way, 1])
    for way, (to, _, mine, other) in enumerate(ways):
        sent[way, 0].wait_recv()
        sums[way] = x_ref[mine, cols(to)] + held[way, 0]
        sent[way, 2] = send(way, 2, sums.at[way], held.at[way, 2])
    for way in range(2):
        sent[way, 1].wait_recv()
        sent[way, 2].wait_recv()
    out_ref[0:half, cols(me)] = x_ref[0:half, cols(me)] + held[0, 2] + held[1, 1]
    out_ref[half:width, cols(me)] = x_ref[half:width, cols(me)] + held[1, 2] + held[0, 1]
    for way, (to, back, mine, other) in enumerate(ways):
        sent[way, 3] = send(way, 3, out_ref.at[mine, cols(me)], out_ref.at[mine, cols(me)])
        sent[way, 4] = send(way, 4, out_ref.at[other, cols(me)], out_ref.at[other, cols(me)])
    for way, (to, back, mine, other) in enumerate(ways):
        sent[way, 3].wait_recv()
        sent[way, 5] = send(way, 5, out_ref.at[mine, cols(back)], out_ref.at[mine, cols(back)])
    for way in range(2):
        sent[way, 4].wait_recv()
        sent[way, 5].wait_recv()
    for copy in sent.values():
        copy.wait_send()


def remote_call(kernel, n, outs, scratch, collective_id, flops, moved):
    return pl.pallas_call(
        functools.partial(kernel, n),
        out_shape=outs,
        in_specs=[pl.BlockSpec(memory_space=pltpu.VMEM)],
        out_specs=pl.BlockSpec(memory_space=pltpu.VMEM),
        scratch_shapes=scratch,
        compiler_params=pltpu.CompilerParams(
            collective_id=collective_id, has_side_effects=True, vmem_limit_bytes=40 << 20),
        cost_estimate=pl.CostEstimate(flops=flops, bytes_accessed=moved, transcendentals=0),
        name=kernel.__name__.removesuffix("_kernel"),
    )


DMA = pltpu.SemaphoreType.DMA


def body(embeddings, rel_weight, head_row, rel_id, tail_owner, tail_row, neg_owner, neg_row):
    peers, n = lax.axis_size("dom"), lax.axis_size("rel")
    me = lax.axis_index("rel")
    rows, width = embeddings.shape
    edges, negs = head_row.shape[0], neg_row.shape[0]
    groups = rel_weight.shape[0]
    quarter = negs // n
    lists = WIDE
    spare = jnp.full((lists - edges - quarter,), 255, I32)
    own_owner = lax.dynamic_slice(neg_owner[:, 0], (me * quarter,), (quarter,))
    own_row = lax.dynamic_slice(neg_row, (me * quarter,), (quarter,))
    owners = jnp.concatenate([tail_owner[:, 0], own_owner + 64, spare]).reshape(1, lists)
    rows_asked = jnp.concatenate([tail_row, own_row, spare]).reshape(1, lists)
    et = embeddings.T
    head = head_row.reshape(1, edges)
    rel = rel_id.reshape(1, edges)

    ids, slot = local_call(route_kernel, (shape(peers, 128, dtype=I32), shape(1, lists, dtype=I32)))(owners, rows_asked)
    asked = lax.all_to_all(ids.reshape(peers, 1, 128), "dom", 0, 0, tiled=True).reshape(peers, 128)
    table = pltpu.VMEM((WIDE, rows), BF16)
    block = shape(peers, SLOTS, MAIN)
    served = local_call(serve_kernel, block, [table] * 3, flops=int(7e9), moved=5 << 20)(asked, et)
    got = lax.all_to_all(served, "dom", 0, 0, tiled=True)
    head_emb, rel_rows = local_call(
        heads_kernel, (shape(edges, WIDE), shape(edges, WIDE)), [table] * 3, flops=int(3e9), moved=5 << 20
    )(head, rel, et, rel_weight)
    tail_emb, neg_part = local_call(unpack_kernel, (shape(edges, WIDE), shape(quarter, WIDE)))(slot, got)
    neg_emb = remote_call(
        gather_kernel, n, shape(n, quarter, WIDE), [DMA((n - 1,)), DMA((n - 1,)), DMA(())], 0, 0, 1 << 20
    )(neg_part).reshape(negs, WIDE)
    gh, gt, gn, gr = local_call(
        grads_kernel, (shape(edges, WIDE), shape(edges, WIDE), shape(negs, WIDE), shape(groups, WIDE))
    )(head_emb, rel_rows, tail_emb, neg_emb, rel)
    gn_sum = remote_call(
        reduce_kernel, n, shape(quarter, WIDE),
        [pltpu.VMEM((n - 1, quarter, WIDE), F32), DMA((n - 1,)), DMA((n - 1,))], 1, 0, 1 << 20
    )(gn.reshape(n, quarter, WIDE))
    back = local_call(pack_kernel, block)(slot, gt, gn_sum)
    recv = lax.all_to_all(back, "dom", 0, 0, tiled=True)
    slab = local_call(
        scatter_kernel, shape(width, rows), [pltpu.VMEM((WIDE, peers * SLOTS + edges), BF16)] * 2,
        flops=int(6e9), moved=6 << 20,
    )(asked, recv, gh, head)
    piece, half = rows // n, width // 2
    total = remote_call(
        all_reduce_kernel, n, shape(width, rows),
        [pltpu.VMEM((2, 3, half, piece), F32), pltpu.VMEM((2, half, piece), F32), DMA((2, 6)), DMA((2, 6))], 2, 0, 10 << 20
    )(slab)
    rel_parts = lax.all_to_all(gr.reshape(peers, groups // peers, WIDE), "dom", 0, 0, tiled=True)
    rel_sum = jnp.sum(rel_parts, axis=0)
    relation = lax.all_gather(rel_sum, "dom", axis=0, tiled=True)[:, 0:width]
    return (total.T, relation)


def solution(mesh):
    return jax.shard_map(
        body,
        mesh=mesh,
        in_specs=(
            P("dom", None),
            P("rel", None),
            P(("dom", "rel")),
            P(("dom", "rel")),
            P(("dom", "rel"), None),
            P(("dom", "rel")),
            P("dom", None),
            P("dom"),
        ),
        out_specs=(P("dom", None), P("rel", None)),
        check_vma=False,
    )
```

time: 603 us -> 287 us (0.48); the launches traced: 592 us -> 285 us
  waiting for transfers between devices: 414 us -> 33.9 us
  Pallas kernels: 0 us -> 117 us
  blocking collectives: 0 us -> 100 us
  local copies, waits for them, and re-layouts: 64.5 us -> 8.67 us
  other arithmetic: 42.6 us -> 2.33 us
  starting transfers between devices: 48.9 us -> 21.6 us
  between operations: 14.6 us -> 0.79 us
  matrix products: 7.26 us -> 0 us
    psum x2 -> x0, waiting for transfers between devices: 261 us -> none  [the longest x1 172 us: body(): relation_grad = lax.psum(rel_local, 'dom')]
    all_to_all x6 -> x3, waiting for transfers between devices: 152 us -> 33.9 us  [the longest x1 33.9 us: body(): got = lax.all_to_all(served, 'dom', 0, 0, tiled=True)]
    pallas_call x0 -> x10, Pallas kernels: none -> 117 us  [the longest x1 59.8 us: body(): remote_call(all_reduce_kernel, n, shape(width, rows), [pltpu.VMEM((2, 3,...]
    all_gather x0 -> x1, blocking collectives: none -> 78.8 us  [body(): relation = lax.all_gather(rel_sum, 'dom', axis=0, tiled=True)[:, 0:width]]
    scatter-add x4 -> x0, other arithmetic: 29.8 us -> none  [the longest x1 10.7 us: body(): slab_grad.at[asked_tail.reshape(-1)].add(recv_tail.reshape(-1, width))]
    all_to_all x6 -> x3, starting transfers between devices: 48.5 us -> 21.6 us  [the longest x1 10.6 us: body(): recv = lax.all_to_all(back, 'dom', 0, 0, tiled=True)]
    all_to_all x0 -> x1, blocking collectives: none -> 21.5 us  [body(): lax.all_to_all(ids.reshape(peers, 1, 128), 'dom', 0, 0, tiled=True)]
    gather x6 -> x0, local copies, waits for them, and re-layouts: 21 us -> none  [the longest x2 10.6 us: serve(): embeddings[asked.reshape(-1)].reshape(asked.shape[0], asked.shape[1], width)]
  transfers between devices with their start and end apart: 8 -> 3, of which waited for: 7 -> 1; matrix products, arithmetic and copies ran while one was open for 14% -> 0% of each run, Pallas kernels for 0% -> 7%
where the time goes in v1:
time: 287 us; the launch traced here: 285 us
  Pallas kernels  117 us (41%)
  blocking collectives  100 us (35%)
  waiting for transfers between devices  33.9 us (12%)
  starting transfers between devices  21.6 us (8%)
  local copies, waits for them, and re-layouts  8.67 us (3%)
    all_gather x1, blocking collectives, body(): relation = lax.all_gather(rel_sum, 'dom', axis=0, tiled=True)[:, 0:width]  78.8 us
    pallas_call x1, Pallas kernels, body(): remote_call(all_reduce_kernel, n, shape(width, rows), [pltpu.VMEM((2, 3,...  59.8 us
    all_to_all x1, waiting for transfers between devices, body(): got = lax.all_to_all(served, 'dom', 0, 0, tiled=True)  33.9 us
    all_to_all x1, blocking collectives, body(): lax.all_to_all(ids.reshape(peers, 1, 128), 'dom', 0, 0, tiled=True)  21.5 us
    pallas_call x1, Pallas kernels, body(): remote_call(reduce_kernel, n, shape(quarter, WIDE), [pltpu.VMEM((n - 1, q...  12.8 us
    pallas_call x1, Pallas kernels, body(): remote_call(gather_kernel, n, shape(n, quarter, WIDE), [DMA((n - 1,)), DM...  10.8 us
    all_to_all x1, starting transfers between devices, body(): recv = lax.all_to_all(back, 'dom', 0, 0, tiled=True)  10.6 us
    pallas_call x1, Pallas kernels, body(): local_call(serve_kernel, block, [table] * 3, flops=int(7000000000.0), mov...  9.47 us
  transfers between devices with their start and end apart: 3, of which 1 were waited for; matrix products, arithmetic and copies ran while one was open for 0% of the time, Pallas kernels for 7%

profile of v1, /device:TPU:2, one launch (start us, length us, event | category | flops | bytes accessed | tf_op | source)
XLA Modules:
  0.0 284.8 jit_solution(3027665915018396669)
XLA Ops:
  0.6 0.8 add_bitcast_fusion
  1.4 0.8 dynamic_slice.7
  2.1 0.7 reduce.2
  2.9 0.8 pad_add_fusion
  4.3 21.5 %all_to_all.20 = s32[64,1,128]{2,1,0:T(1,128)S(1)} all-to-all(s32[64,1,128]{2,1,0:T(1,128)S(1)} %bitcast.24), channel_id=1, replica_groups=mesh['dom'=64,'rel'=4] {'dom'}, dimensions={0} | all-to-all | bytes 65536 | tf_op jit(solution)/shard_map/all_to_all | solution.py:376
  25.8 1.9 copy-done
  27.7 9.5 %serve.1 = f32[64,16,384]{2,1,0:T(8,128)} custom-call(s32[64,128]{1,0:T(8,128)S(1)} %bitcast.22, f32[400,2048]{1,0:T(8,128)S(1)} %bitcast.27), custom_call_target="tpu_custom_call" | custom-call | flops 7000000000 | bytes 5242880 | tf_op jit(solution)/shard_map/serve/pallas_call | solution.py:379
  37.2 4.9 %all-to-all-start.1 = ((f32[64,16,384]{2,1,0:T(8,128)}), f32[64,16,384]{2,1,0:T(8,128)S(1)}, u32[]{:S(2)}, u32[]{:S(2)}) async-start(f32[64,16,384]{2,1,0:T(8,128)} %serve.1), calls=%async_computation.1 | async-start | bytes 3145728 | tf_op jit(solution)/shard_map/all_to_all | solution.py:380
  42.1 1.9 copy-done.1
  44.0 4.0 %heads.1 = (f32[384,512]{1,0:T(8,128)S(1)}, f32[384,512]{1,0:T(8,128)S(1)}) custom-call(s32[1,384]{1,0:T(1,128)S(1)} %reshape.39.head_ref, s32[1,384]{1,0:T(1,128)S(1)} %reshape.40.rel_id_ref, f32[400,2048]{1,0:T(8,128)S(1)} %bitcast.28, f32[64,400]{1,0:T(8,128)S(1)} %copy-done.4), custom_call_target="tpu_custom_call" | custom-call | flops 3000000000 | bytes 5242880 | tf_op jit(solution)/shard_map/heads/pallas_call | solution.py:381
  48.1 33.9 %all-to-all-done.1.recv_ref = f32[64,16,384]{2,1,0:T(8,128)S(1)} async-done(((f32[64,16,384]{2,1,0:T(8,128)}), f32[64,16,384]{2,1,0:T(8,128)S(1)}, u32[]{:S(2)}, u32[]{:S(2)}) %all-to-all-start.1) | async-done | bytes 1572896 | tf_op jit(solution)/shard_map/all_to_all | solution.py:380
  82.0 2.9 %unpack.1 = (f32[384,512]{1,0:T(8,128)S(1)}, f32[96,512]{1,0:T(8,128)S(1)}) custom-call(s32[1,512]{1,0:T(1,128)S(1)} %get-tuple-element.13.slot_ref, f32[64,16,384]{2,1,0:T(8,128)S(1)} %all-to-all-done.1.recv_ref), custom_call_target="tpu_custom_call" | custom-call | tf_op jit(solution)/shard_map/unpack/pallas_call | solution.py:384
  84.9 10.8 %gather.1 = f32[4,96,512]{2,1,0:T(8,128)S(1)} custom-call(f32[96,512]{1,0:T(8,128)S(1)} %get-tuple-element.17.in_ref), custom_call_target="tpu_custom_call" | custom-call | bytes 1048576 | tf_op jit(solution)/shard_map/gather/pallas_call | solution.py:385
  95.7 4.3 %grads.1 = (f32[384,512]{1,0:T(8,128)S(1)}, f32[384,512]{1,0:T(8,128)S(1)}, f32[384,512]{1,0:T(8,128)S(1)}, f32[64,512]{1,0:T(8,128)S(1)}) custom-call(f32[384,512]{1,0:T(8,128)S(1)} %get-tuple-element.14.head_ref, f32[384,512]{1,0:T(8,128)S(1)} %get-tuple-element.15.relrow_ref, f32[384,512]{1,0:T(8,128)S(1)} %get-tuple-element.16.tail_ref, ...), custom_call_target="tpu_custom_call" | custom-call | tf_op jit(solution)/shard_map/grads/pallas_call | solution.py:388
  100.1 0.9 copy-done.2
  100.9 0.8 copy.11
  101.7 6.1 %all-to-all-start.3 = ((f32[64,1,512]{2,1,0:T(1,128)}), f32[64,1,512]{2,1,0:T(1,128)S(1)}, u32[]{:S(2)}, u32[]{:S(2)}) async-start(f32[64,1,512]{2,1,0:T(1,128)} %copy.11), calls=%async_computation.3 | async-start | bytes 262144 | tf_op jit(solution)/shard_map/all_to_all | solution.py:406
  107.8 12.8 %reduce.3.gn_ref = f32[96,512]{1,0:T(8,128)S(1)} custom-call(f32[4,96,512]{2,1,0:T(8,128)S(1)} %bitcast.20), custom_call_target="tpu_custom_call" | custom-call | bytes 1048576 | tf_op jit(solution)/shard_map/reduce/pallas_call | solution.py:391
  120.7 3.7 %pack.1 = f32[64,16,384]{2,1,0:T(8,128)} custom-call(s32[1,512]{1,0:T(1,128)S(1)} %get-tuple-element.13.slot_ref, f32[384,512]{1,0:T(8,128)S(1)} %get-tuple-element.18.gt_ref, f32[96,512]{1,0:T(8,128)S(1)} %reduce.3.gn_ref), custom_call_target="tpu_custom_call" | custom-call | tf_op jit(solution)/shard_map/pack/pallas_call | solution.py:395
  124.4 10.6 %all-to-all-start.2 = ((f32[64,16,384]{2,1,0:T(8,128)}), f32[64,16,384]{2,1,0:T(8,128)S(1)}, u32[]{:S(2)}, u32[]{:S(2)}) async-start(f32[64,16,384]{2,1,0:T(8,128)} %pack.1), calls=%async_computation.2 | async-start | bytes 3145728 | tf_op jit(solution)/shard_map/all_to_all | solution.py:396
  135.1 78.8 %all-gather.1 = f32[64,1,512]{2,1,0:T(1,128)S(1)} all-gather(f32[1,1,512]{2,1,0:T(1,128)S(1)} %bitcast.30), channel_id=2, replica_groups=mesh['dom'=64,'rel'=4] {'dom'}, dimensions={0}, use_global_device_ids=true | all-gather | bytes 133120 | tf_op jit(solution)/shard_map/all_gather | solution.py:408
  214.6 8.6 %scatter.1.x_ref = f32[400,2048]{1,0:T(8,128)S(1)} custom-call(s32[64,128]{1,0:T(8,128)S(1)} %bitcast.23, f32[64,16,384]{2,1,0:T(8,128)S(1)} %all-to-all-done.2.recv_ref, f32[384,512]{1,0:T(8,128)S(1)} %copy-done.3, s32[1,384]{1,0:T(1,128)S(1)} %reshape.39.head_ref), custom_call_target="tpu_custom_call" | custom-call | flops 6000000000 | bytes 6291456 | tf_op jit(solution)/shard_map/scatter/pallas_call | solution.py:397
  223.2 59.8 %all_reduce.1 = f32[400,2048]{1,0:T(8,128)S(1)} custom-call(f32[400,2048]{1,0:T(8,128)S(1)} %scatter.1.x_ref), custom_call_target="tpu_custom_call" | custom-call | bytes 10485760 | tf_op jit(solution)/shard_map/all_reduce/pallas_call | solution.py:402
  283.0 1.7 copy.16
  (19 shorter events, 1.5 us)
Async XLA Ops:
  25.8 1.9 copy-start
  27.7 14.3 %copy-start.5 = (s32[384]{0:T(512)S(1)}, s32[384]{0:T(512)}, u32[]{:S(2)}) copy-start(s32[384]{0:T(512)} %param.10) | copy-start | bytes 4612
  27.7 14.4 %copy-start.6 = (s32[384]{0:T(512)S(1)}, s32[384]{0:T(512)}, u32[]{:S(2)}) copy-start(s32[384]{0:T(512)} %param.11) | copy-start | bytes 4612
  27.7 14.4 %copy-start.4 = (f32[64,400]{1,0:T(8,128)S(1)}, f32[64,400]{1,0:T(8,128)}, u32[]{:S(2)}) copy-start(f32[64,400]{1,0:T(8,128)} %rel_ref.1) | copy-start | bytes 307204
  37.2 44.8 %all-to-all-start.1 = ((f32[64,16,384]{2,1,0:T(8,128)}), f32[64,16,384]{2,1,0:T(8,128)S(1)}, u32[]{:S(2)}, u32[]{:S(2)}) async-start(f32[64,16,384]{2,1,0:T(8,128)} %serve.1), calls=%async_computation.1 | async-start | bytes 3145728 | tf_op jit(solution)/shard_map/all_to_all | solution.py:380
  42.1 1.9 copy-start.1
  100.0 0.9 copy-start.2
  101.7 22.6 %all-to-all-start.3 = ((f32[64,1,512]{2,1,0:T(1,128)}), f32[64,1,512]{2,1,0:T(1,128)S(1)}, u32[]{:S(2)}, u32[]{:S(2)}) async-start(f32[64,1,512]{2,1,0:T(1,128)} %copy.11), calls=%async_computation.3 | async-start | bytes 262144 | tf_op jit(solution)/shard_map/all_to_all | solution.py:406
  120.7 93.9 %copy-start.3 = (f32[384,512]{1,0:T(8,128)S(1)}, f32[384,512]{1,0:T(8,128)}, u32[]{:S(2)}) copy-start(f32[384,512]{1,0:T(8,128)} %copy-done.2) | copy-start | bytes 2359300
  124.4 90.2 %all-to-all-start.2 = ((f32[64,16,384]{2,1,0:T(8,128)}), f32[64,16,384]{2,1,0:T(8,128)S(1)}, u32[]{:S(2)}, u32[]{:S(2)}) async-start(f32[64,16,384]{2,1,0:T(8,128)} %pack.1), calls=%async_computation.2 | async-start | bytes 3145728 | tf_op jit(solution)/shard_map/all_to_all | solution.py:396

commit v2 on v0

v2 whole, which is shorter than its diff:
```python
import jax
import jax.numpy as jnp
from jax import lax
from jax.experimental import pallas as pl
from jax.experimental.pallas import tpu as pltpu
from jax.sharding import PartitionSpec as P

SPAN = 128
MAIN = 384
WIDE = 512
SLOTS = 16
CAP_T = 12
F32, BF16, I32 = jnp.float32, jnp.bfloat16, jnp.int32
MESH = pl.DeviceIdType.MESH
HIGHEST = lax.Precision.HIGHEST
NN = (((1,), (0,)), ((), ()))
NT = (((1,), (1,)), ((), ()))
TN = (((0,), (0,)), ((), ()))


def iota(shape, dim):
    return lax.broadcasted_iota(I32, shape, dim)


def parts(x, count):
    out = []
    for _ in range(count - 1):
        hi = x.astype(BF16)
        out.append(hi)
        x = x - hi.astype(F32)
    return out + [x.astype(BF16)]


def dot(a, b, dims):
    return lax.dot_general(a, b, dims, preferred_element_type=F32)


def dot_parts(onehot, values, dims=NN):
    total = dot(onehot, values[0], dims)
    for v in values[1:]:
        total = total + dot(onehot, v, dims)
    return total


def column(row):
    n = row.shape[1]
    return jnp.broadcast_to(row.astype(F32), (8, n)).T[:, 0:1].astype(I32)


def onehot(mask):
    return jnp.where(mask, 1.0, 0.0).astype(BF16)


def fold_matrix(rows, cols):
    l, m = iota((rows, cols), 0), iota((rows, cols), 1)
    return onehot((l & 15) == m)


def spread_matrix(rows, cols):
    m, l = iota((rows, cols), 0), iota((rows, cols), 1)
    return onehot((l & 15) == m)


def steps(i):
    j, q = lax.div(i, 8), 7 - lax.rem(i, 8)
    t, odd = lax.div(j, 2), lax.rem(j, 2)
    return (1 - odd) * (4 - t) + odd * lax.rem(5 + t, 8), lax.div(q, 2), lax.rem(q, 2)


def plus(me, i):
    dz, dy, dc = steps(i)
    z, y, c = lax.div(me, 8), lax.rem(lax.div(me, 2), 4), lax.rem(me, 2)
    return lax.rem(z + dz, 8) * 8 + lax.rem(y + dy, 4) * 2 + lax.rem(c + dc, 2)


def minus(me, i):
    dz, dy, dc = steps(i)
    z, y, c = lax.div(me, 8), lax.rem(lax.div(me, 2), 4), lax.rem(me, 2)
    return lax.rem(z + 8 - dz, 8) * 8 + lax.rem(y + 4 - dy, 4) * 2 + lax.rem(c + dc, 2)


def number(me, owner):
    z, y, c = lax.div(me, 8), lax.rem(lax.div(me, 2), 4), lax.rem(me, 2)
    dz = ((owner >> 3) - z + 8) & 7
    dz = jnp.where(dz == 0, 8, dz)
    j = jnp.where(dz <= 4, 8 - 2 * dz, 2 * dz - 9)
    dy = (((owner >> 1) & 3) - y + 4) & 3
    dc = ((owner & 1) - c + 2) & 1
    return j * 8 + 7 - (dy * 2 + dc)


def id_column(ids):
    p = ids.shape[0]
    spread = jnp.broadcast_to(ids.astype(F32), (p, SLOTS, 128))
    own = iota((p, SLOTS, 128), 1) == iota((p, SLOTS, 128), 2)
    return jnp.sum(jnp.where(own, spread, 0.0), axis=2, keepdims=True).reshape(p * SLOTS, 1).astype(I32)


GROUP = 16
CHUNKS = 3


def kernel(
    towner_ref, trow_ref, nowner_ref, nrow_ref, head_ref, rel_id_ref, rel_ref, et_hbm,
    out_ref, rel_out,
    et_ref, hi_ref, mid_ref, lo_ref, oh_ref, ids_ref, asked_ref, served_ref, fetched_ref, got_ref, negs_ref,
    head_emb, rel_rows, gh_ref, gt_ref, gn_ref, gn_held, back_ref, recv_ref, vt_hi, vt_lo, slab_ref, held_ref, sums_ref,
    gr_ref, gr_recv, gr_sum,
    et_sem, ids_send, ids_recv, serve_send, serve_recv, neg_send, neg_recv, gn_send, gn_recv, back_send, back_recv,
    gr_send, gr_got, ag_send, ag_recv, ring_send, ring_recv,
):
    peers = ids_ref.shape[0]
    others = peers - 1
    n = negs_ref.shape[0]
    me, g = lax.axis_index("dom"), lax.axis_index("rel")
    edges, negs = head_ref.shape[1], nowner_ref.shape[1]
    quarter = negs // n
    lists = WIDE
    slots = peers * SLOTS
    width, rows = et_ref.shape
    tables = (hi_ref, mid_ref, lo_ref)

    load = pltpu.make_async_copy(et_hbm, et_ref, et_sem)
    load.start()
    barrier = pltpu.get_barrier_semaphore()

    @pl.loop(0, others)
    def _(i):
        pl.semaphore_signal(barrier, inc=1, device_id={"dom": plus(me, i)}, device_id_type=MESH)

    for k in range(1, n):
        pl.semaphore_signal(barrier, inc=1, device_id={"rel": lax.rem(g + k, n)}, device_id_type=MESH)

    def mine(ref):
        return sum(jnp.where(g == q, ref[:, quarter * q : quarter * (q + 1)], 0) for q in range(n))

    spare = jnp.zeros((1, lists - edges - quarter), I32)
    owner = jnp.concatenate([towner_ref[...], mine(nowner_ref) + 64, spare + 255], axis=1)
    asked_rows = jnp.concatenate([trow_ref[...], mine(nrow_ref), spare], axis=1)
    same = column(owner) == owner
    earlier = iota((lists, lists), 0) < iota((lists, lists), 1)
    position = jnp.sum(jnp.where(same & earlier, 1.0, 0.0), axis=0, keepdims=True).astype(I32)
    negative, valid = owner >= 64, owner < 128
    position = jnp.where(negative, position + CAP_T, position)
    peer = number(me, owner & 63)
    slot = jnp.where(valid, peer * SLOTS + position, -1)
    left = jnp.where((iota((peers, lists), 0) == peer) & valid, (asked_rows + 1).astype(F32), 0.0)
    right = jnp.where(iota((128, lists), 0) == position, 1.0, 0.0)
    ids = lax.dot_general(left, right, NT, precision=HIGHEST, preferred_element_type=F32)
    ids_ref[...] = ((ids + 0.5).astype(I32) - 1)[:, None, :]

    pl.semaphore_wait(barrier, others + n - 1)

    def dom_copy(src, dst, send, recv, device):
        return pltpu.make_async_remote_copy(
            src, dst, send, recv, device_id={"dom": device}, device_id_type=MESH)

    @pl.loop(0, others)
    def _(i):
        dom_copy(ids_ref.at[i], asked_ref.at[i], ids_send, ids_recv, plus(me, i)).start()

    pltpu.make_async_copy(ids_ref.at[others], asked_ref.at[others], ids_recv).start()

    load.wait()

    @pl.loop(0, width // 16)
    def _(i):
        at = pl.multiple_of(i * 16, 16)
        for t, v in zip(tables, parts(et_ref[pl.ds(at, 16), :], 3), strict=True):
            t[pl.ds(at, 16), :] = v

    for t in tables:
        for k in range(1, 8):
            t[MAIN + 16 * k : MAIN + 16 * (k + 1), :] = t[MAIN : MAIN + 16, :]

    pltpu.make_async_copy(ids_ref, asked_ref, ids_recv).wait()

    @pl.loop(0, peers // GROUP)
    def _(b):
        at = pl.multiple_of(b * GROUP, GROUP)
        col = id_column(asked_ref[pl.ds(at, GROUP)])
        hot = onehot(iota((GROUP * SLOTS, rows), 1) == col)
        oh_ref[pl.ds(pl.multiple_of(b * GROUP * SLOTS, GROUP * SLOTS), GROUP * SLOTS), :] = hot
        got = dot_parts(hot, [t[...] for t in tables], NT)
        place = iota((GROUP, SLOTS, 128), 1)
        lane = iota((GROUP, SLOTS, 128), 2)
        rest = got[:, MAIN:].reshape(GROUP, SLOTS, 128)
        rest = jnp.where((lane >> 4) == (place & 7), rest, 0.0)
        low = jnp.sum(jnp.where(place < 8, rest, 0.0), axis=1, keepdims=True)
        high = jnp.sum(jnp.where(place < 8, 0.0, rest), axis=1, keepdims=True)
        for k, part in enumerate((low, high, jnp.zeros_like(low))):
            main = got[:, 128 * k : 128 * (k + 1)].reshape(GROUP, SLOTS, 128)
            served_ref[pl.ds(at, GROUP), :, 128 * k : 128 * (k + 1)] = jnp.where(place == SLOTS - 1, part, main)

        @pl.loop(0, GROUP)
        def _(k):
            i = b * GROUP + k

            @pl.when(i < others)
            def _():
                dom_copy(served_ref.at[i], fetched_ref.at[i], serve_send, serve_recv.at[b], minus(me, i)).start()

    last = peers // GROUP - 1
    pltpu.make_async_copy(served_ref.at[others], fetched_ref.at[others], serve_recv.at[last]).start()

    hot = onehot(iota((edges, rows), 1) == column(head_ref[...]))
    oh_ref[slots:, :] = hot
    got = dot_parts(hot, [t[...] for t in tables], NT)
    head_emb[:, 0:MAIN] = got[:, 0:MAIN]
    head_emb[:, MAIN:WIDE] = jnp.where(iota((edges, 128), 1) < width - MAIN, got[:, MAIN:WIDE], 0.0)
    groups = rel_ref.shape[0]
    hot = onehot(iota((edges, groups), 1) == column(rel_id_ref[...]))
    rel_rows[:, 0:width] = dot_parts(hot, parts(rel_ref[...], 3))
    rel_rows[:, width:WIDE] = jnp.zeros((edges, WIDE - width), F32)

    slot_col = column(slot)
    got_ref[...] = jnp.zeros_like(got_ref)

    @pl.loop(0, peers // GROUP)
    def _(b):
        at = pl.ds(pl.multiple_of(b * GROUP, GROUP), GROUP)
        pltpu.make_async_copy(served_ref.at[at], fetched_ref.at[at], serve_recv.at[b]).wait()
        hot = onehot(iota((lists, GROUP * SLOTS), 1) + b * (GROUP * SLOTS) == slot_col)
        got_ref[:, 0:MAIN] += dot_parts(hot, parts(fetched_ref[at].reshape(GROUP * SLOTS, MAIN), 3))

    hot_peer = onehot(iota((lists, peers), 1) == (slot_col >> 4))
    rest = dot_parts(hot_peer, parts(fetched_ref[:, SLOTS - 1, 0:256], 3))
    rest = jnp.where((iota((lists, 256), 1) >> 4) == (slot_col & 15), rest, 0.0)
    fold = fold_matrix(256, 128)
    got_ref[:, MAIN:WIDE] = sum(dot(p, fold, NN) for p in parts(rest, 3))

    negs_ref[g] = got_ref[edges : edges + quarter, :]

    def rel_copy(src, dst, send, recv, k):
        return pltpu.make_async_remote_copy(
            src, dst, send, recv, device_id={"rel": lax.rem(g + k, n)}, device_id_type=MESH)

    copies = [rel_copy(negs_ref.at[g], negs_ref.at[g], neg_send.at[k - 1], neg_recv.at[k - 1], k) for k in range(1, n)]
    for copy in copies:
        copy.start()
    for copy in copies:
        copy.wait_recv()
    sent = list(copies)

    def neg_rows(c):
        return negs_ref[...].reshape(negs, WIDE)[c * SPAN : (c + 1) * SPAN]

    gn_parts = []
    for c in range(edges // SPAN):
        at = slice(c * SPAN, (c + 1) * SPAN)
        head, rel, tail, neg = head_emb[at], rel_rows[at], got_ref[at], neg_rows(c)
        queries = head * rel
        positive = jnp.sum(queries * tail, axis=1, keepdims=True)
        scores = lax.dot_general(queries, neg, NT, precision=HIGHEST, preferred_element_type=F32)
        row_max = jnp.maximum(positive, jnp.max(scores, axis=1, keepdims=True))
        pos_exp = jnp.exp(positive - row_max)
        neg_exp = jnp.exp(scores - row_max)
        total = pos_exp + jnp.sum(neg_exp, axis=1, keepdims=True)
        pos_coef = pos_exp / total - 1.0
        neg_coef = neg_exp / total
        grad_query = pos_coef * tail + lax.dot_general(
            neg_coef, neg, NN, precision=HIGHEST, preferred_element_type=F32)
        gh_ref[at] = grad_query * rel
        gt_ref[at] = pos_coef * queries
        grad_neg = lax.dot_general(neg_coef.T, queries, NN, precision=HIGHEST, preferred_element_type=F32)
        first = c * SPAN
        while first < (c + 1) * SPAN:
            q, inside = divmod(first, quarter)
            count = min(quarter - inside, (c + 1) * SPAN - first)
            gn_ref[q, inside : inside + count] = grad_neg[first - c * SPAN : first - c * SPAN + count]
            first += count
        hot = onehot(iota((groups, SPAN), 0) == rel_id_ref[:, at])
        part = dot_parts(hot, parts(grad_query * head, 3))
        gn_parts.append(part)
    gr_ref[...] = sum(gn_parts)[:, None, :]

    copies = [
        rel_copy(gn_ref.at[lax.rem(g + k, n)], gn_held.at[k - 1], gn_send.at[k - 1], gn_recv.at[k - 1], k) for k in range(1, n)
    ]
    for copy in copies:
        copy.start()

    @pl.loop(0, others)
    def _(i):
        to = plus(me, i)
        dom_copy(gr_ref.at[to], gr_recv.at[i], gr_send, gr_got, to).start()

    pltpu.make_async_copy(gr_ref.at[me], gr_recv.at[others], gr_got).start()

    hot = onehot(iota((slots, lists), 0) == slot)
    hot_peer = onehot(iota((peers, lists), 0) == (slot >> 4))
    for copy in copies:
        copy.wait_recv()
    sent += copies
    grad_neg = gn_ref[g] + gn_held[0] + gn_held[1] + gn_held[2]
    values = jnp.concatenate([gt_ref[...], grad_neg, jnp.zeros((lists - edges - quarter, WIDE), F32)], axis=0)
    rest = sum(dot(p, spread_matrix(128, 256), NN) for p in parts(values[:, MAIN:WIDE], 3))
    rest = jnp.where((iota((lists, 256), 1) >> 4) == (slot_col & 15), rest, 0.0)
    rest = dot_parts(hot_peer, parts(rest, 3))
    place = iota((peers, SLOTS, 128), 1)
    for k in range(CHUNKS):
        main = dot_parts(hot, parts(values[:, 128 * k : 128 * (k + 1)], 2)).reshape(peers, SLOTS, 128)
        if k < 2:
            main = jnp.where(place == SLOTS - 1, rest[:, 128 * k : 128 * (k + 1)][:, None, :], main)
        back_ref[k] = main

        @pl.loop(0, others)
        def _(i, k=k):
            dom_copy(back_ref.at[k, i], recv_ref.at[k, i], back_send, back_recv.at[k], plus(me, i)).start()

        pltpu.make_async_copy(back_ref.at[k, others], recv_ref.at[k, others], back_recv.at[k]).start()

    piece = rows // n
    right_hand, left_hand, far = lax.rem(g + 1, n), lax.rem(g + 3, n), lax.rem(g + 2, n)
    first_row = [128 * k for k in range(CHUNKS)]
    height = [128] * (CHUNKS - 1) + [width - 128 * (CHUNKS - 1)]

    def cols(j):
        return pl.ds(pl.multiple_of(j * piece, piece), piece)

    ring = {}
    to_of, back_of = (right_hand, left_hand), (left_hand, right_hand)

    def half(k, way, mine):
        h = height[k] // 2
        low = (way == 0) == mine
        return slice(first_row[k], first_row[k] + h) if low else slice(first_row[k] + h, first_row[k] + 2 * h)

    def send(k, way, step, src, dst):
        copy = pltpu.make_async_remote_copy(
            src, dst, ring_send.at[k, way, step], ring_recv.at[k, way, step],
            device_id={"rel": to_of[way]}, device_id_type=MESH)
        copy.start()
        ring[k, way, step] = copy

    def scatter(k):
        pltpu.make_async_copy(back_ref.at[k], recv_ref.at[k], back_recv.at[k]).wait()
        values = [recv_ref[k].reshape(slots, 128).T, gh_ref[:, 128 * k : 128 * (k + 1)].T]
        vt = jnp.concatenate(values, axis=1)
        if k == CHUNKS - 1:
            rest = jnp.concatenate([recv_ref[0, :, SLOTS - 1, :], recv_ref[1, :, SLOTS - 1, :]], axis=1)
            rest = jnp.broadcast_to(rest[:, None, :], (peers, SLOTS, 256))
            own = (iota((peers, SLOTS, 256), 2) >> 4) == iota((peers, SLOTS, 256), 1)
            rest = jnp.where(own, rest, 0.0).reshape(slots, 256)
            rest = sum(dot(p, fold, NN) for p in parts(rest, 2))
            more = jnp.concatenate([rest.T[0:16], gh_ref[:, MAIN:WIDE].T[0:16]], axis=1)
            vt = jnp.concatenate([vt, more], axis=0)
        h = height[k]
        vt_hi[0:h], vt_lo[0:h] = parts(vt, 2)

        @pl.loop(0, n)
        def _(j):
            at = cols(j)
            slab_ref[first_row[k] : first_row[k] + h, at] = dot(vt_hi[0:h], oh_ref[:, at], NN) + dot(
                vt_lo[0:h], oh_ref[:, at], NN)

    def begin(k):
        h = height[k] // 2
        for way in range(2):
            send(k, way, 0, slab_ref.at[half(k, way, True), cols(far)], held_ref.at[k, way, 0, 0:h])
            send(k, way, 1, slab_ref.at[half(k, way, False), cols(to_of[way])], held_ref.at[k, way, 1, 0:h])

    def add(k):
        h = height[k] // 2
        for way in range(2):
            ring[k, way, 0].wait_recv()
            sums_ref[k, way, 0:h] = slab_ref[half(k, way, True), cols(to_of[way])] + held_ref[k, way, 0, 0:h]
            send(k, way, 2, sums_ref.at[k, way, 0:h], held_ref.at[k, way, 2, 0:h])

    def share(k):
        h = height[k] // 2
        for way in range(2):
            ring[k, way, 1].wait_recv()
            ring[k, way, 2].wait_recv()
        for way in range(2):
            at = half(k, way, True)
            out_ref[at, cols(g)] = slab_ref[at, cols(g)] + held_ref[k, way, 2, 0:h] + held_ref[k, 1 - way, 1, 0:h]
        for way in range(2):
            for step, mine_too in ((3, True), (4, False)):
                at = half(k, way, mine_too)
                send(k, way, step, out_ref.at[at, cols(g)], out_ref.at[at, cols(g)])

    def forward(k):
        for way in range(2):
            ring[k, way, 3].wait_recv()
            at = half(k, way, True)
            send(k, way, 5, out_ref.at[at, cols(back_of[way])], out_ref.at[at, cols(back_of[way])])

    scatter(0)
    begin(0)
    pltpu.make_async_copy(gr_ref, gr_recv, gr_got).wait()
    gr_sum[0] = jnp.sum(gr_recv[...], axis=0)

    @pl.loop(0, others)
    def _(i):
        dom_copy(gr_sum.at[0], rel_out.at[me], ag_send, ag_recv, plus(me, i)).start()

    pltpu.make_async_copy(gr_sum.at[0], rel_out.at[me], ag_recv).start()
    add(0)
    scatter(1)
    begin(1)
    share(0)
    add(1)
    scatter(2)
    begin(2)
    forward(0)
    share(1)
    add(2)
    forward(1)
    share(2)
    forward(2)
    for k in range(CHUNKS):
        for way in range(2):
            ring[k, way, 4].wait_recv()
            ring[k, way, 5].wait_recv()
    pltpu.make_async_copy(gr_ref, rel_out, ag_recv).wait()

    for copy in [*sent, *ring.values()]:
        copy.wait_send()
    first = pl.ds(0, others)
    pltpu.make_async_copy(ids_ref.at[first], ids_ref.at[first], ids_send).wait()
    pltpu.make_async_copy(served_ref.at[first], served_ref.at[first], serve_send).wait()
    pltpu.make_async_copy(gr_ref.at[first], gr_ref.at[first], gr_send).wait()
    pltpu.make_async_copy(gr_ref.at[first], gr_ref.at[first], ag_send).wait()
    for k in range(CHUNKS):
        pltpu.make_async_copy(back_ref.at[k, first], back_ref.at[k, first], back_send).wait()


def body(embeddings, rel_weight, head_row, rel_id, tail_owner, tail_row, neg_owner, neg_row):
    peers, n = lax.axis_size("dom"), lax.axis_size("rel")
    rows, width = embeddings.shape
    edges, negs = head_row.shape[0], neg_row.shape[0]
    groups = rel_weight.shape[0]
    quarter = negs // n
    lists = WIDE
    slots = peers * SLOTS
    tall = (width - 128 * (CHUNKS - 1)) // 2
    V, DMA = pltpu.VMEM, pltpu.SemaphoreType.DMA
    vmem, anywhere = pl.BlockSpec(memory_space=pltpu.VMEM), pl.BlockSpec(memory_space=pl.ANY)
    scratch = [
        V((width, rows), F32), V((WIDE, rows), BF16), V((WIDE, rows), BF16), V((WIDE, rows), BF16),
        V((slots + edges, rows), BF16), V((peers, 1, 128), I32), V((peers, 1, 128), I32),
        V((peers, SLOTS, MAIN), F32), V((peers, SLOTS, MAIN), F32), V((lists, WIDE), F32), V((n, quarter, WIDE), F32),
        V((edges, WIDE), F32), V((edges, WIDE), F32), V((edges, WIDE), F32), V((edges, WIDE), F32),
        V((n, quarter, WIDE), F32), V((n - 1, quarter, WIDE), F32),
        V((CHUNKS, peers, SLOTS, 128), F32), V((CHUNKS, peers, SLOTS, 128), F32),
        V((2 * tall, slots + edges), BF16), V((2 * tall, slots + edges), BF16),
        V((width, rows), F32), V((CHUNKS, 2, 3, tall, rows // n), F32), V((CHUNKS, 2, tall, rows // n), F32),
        V((groups, 1, WIDE), F32), V((peers, 1, WIDE), F32), V((1, 1, WIDE), F32),
        DMA(()), DMA(()), DMA(()), DMA(()), DMA((peers // GROUP,)), DMA((n - 1,)), DMA((n - 1,)), DMA((n - 1,)), DMA((n - 1,)),
        DMA(()), DMA((CHUNKS,)), DMA(()), DMA(()), DMA(()), DMA(()), DMA((CHUNKS, 2, 6)), DMA((CHUNKS, 2, 6)),
    ]
    total, relation = pl.pallas_call(
        kernel,
        out_shape=(jax.ShapeDtypeStruct((width, rows), F32), jax.ShapeDtypeStruct((groups, 1, WIDE), F32)),
        in_specs=[vmem] * 7 + [anywhere],
        out_specs=(vmem, vmem),
        scratch_shapes=scratch,
        compiler_params=pltpu.CompilerParams(collective_id=0, has_side_effects=True, vmem_limit_bytes=58 << 20),
        cost_estimate=pl.CostEstimate(flops=int(3e10), bytes_accessed=7 << 20, transcendentals=0),
        name="ranking_gradients",
    )(
        tail_owner.reshape(1, edges), tail_row.reshape(1, edges), neg_owner.reshape(1, negs), neg_row.reshape(1, negs),
        head_row.reshape(1, edges), rel_id.reshape(1, edges), rel_weight, embeddings.T)
    return (total.T, relation.reshape(groups, WIDE)[:, 0:width])


def solution(mesh):
    return jax.shard_map(
        body,
        mesh=mesh,
        in_specs=(
            P("dom", None),
            P("rel", None),
            P(("dom", "rel")),
            P(("dom", "rel")),
            P(("dom", "rel"), None),
            P(("dom", "rel")),
            P("dom", None),
            P("dom"),
        ),
        out_specs=(P("dom", None), P("rel", None)),
        check_vma=False,
    )
```

time: 603 us -> 174 us (0.29); the launches traced: 592 us -> 174 us
  waiting for transfers between devices: 414 us -> 0 us
  Pallas kernels: 0 us -> 163 us
  local copies, waits for them, and re-layouts: 64.5 us -> 10.6 us
  starting transfers between devices: 48.9 us -> 0 us
  other arithmetic: 42.6 us -> 0 us
  between operations: 14.6 us -> 0.64 us
  matrix products: 7.26 us -> 0 us
    psum x2 -> x0, waiting for transfers between devices: 261 us -> none  [the longest x1 172 us: body(): relation_grad = lax.psum(rel_local, 'dom')]
    pallas_call x0 -> x1, Pallas kernels: none -> 163 us  [body(): pl.pallas_call(kernel, out_shape=(jax.ShapeDtypeStruct((width, rows), F32...]
    all_to_all x6 -> x0, waiting for transfers between devices: 152 us -> none  [the longest x1 45 us: body(): lax.all_to_all(tail_back, 'dom', split_axis=0, concat_axis=0, tiled=True)]
    all_to_all x6 -> x0, starting transfers between devices: 48.5 us -> none  [the longest x1 12.1 us: body(): lax.all_to_all(tail_ids, 'dom', split_axis=0, concat_axis=0, tiled=True)]
    scatter-add x4 -> x0, other arithmetic: 29.8 us -> none  [the longest x1 10.7 us: body(): slab_grad.at[asked_tail.reshape(-1)].add(recv_tail.reshape(-1, width))]
    gather x6 -> x0, local copies, waits for them, and re-layouts: 21 us -> none  [the longest x2 10.6 us: serve(): embeddings[asked.reshape(-1)].reshape(asked.shape[0], asked.shape[1], width)]
    reshape x17 -> x4, local copies, waits for them, and re-layouts: 18.8 us -> 5.03 us  [the longest x1 1.27 us: body(): rel_id.reshape(1, edges)]
    scatter x3 -> x0, local copies, waits for them, and re-layouts: 8.95 us -> none  [the longest x2 6.15 us: id_buffer(): jnp.zeros((dom_count * capacity,), jnp.int32).at[slot_index].set(rows)]
  transfers between devices with their start and end apart: 8 -> 0, of which waited for: 7 -> 0; matrix products, arithmetic and copies ran while one was open for 14% -> 0% of each run, Pallas kernels for 0% -> 0%
where the time goes in v2:
time: 174 us
  Pallas kernels  163 us (94%)
  local copies, waits for them, and re-layouts  10.6 us (6%)
    pallas_call x1, Pallas kernels, body(): pl.pallas_call(kernel, out_shape=(jax.ShapeDtypeStruct((width, rows), F32...  163 us
    unnamed x2, local copies, waits for them, and re-layouts  5.58 us

profile of v2, /device:TPU:2, one launch (start us, length us, event | category | flops | bytes accessed | tf_op | source)
XLA Modules:
  0.0 173.8 jit_solution(7319581791320998679)
XLA Ops:
  0.6 1.3 reshape.29.head_ref
  1.9 1.3 reshape.30.rel_id_ref
  3.2 1.2 reshape.26.trow_ref
  4.4 1.2 reshape.28.nrow_ref
  5.7 162.5 %ranking_gradients.1 = (f32[400,2048]{1,0:T(8,128)}, f32[64,1,512]{2,1,0:T(1,128)}) custom-call(s32[1,384]{1,0:T(1,128)} %bitcast.11, s32[1,384]{1,0:T(1,128)} %reshape.26.trow_ref, s32[1,384]{1,0:T(1,128)} %bitcast.12, s32[1,384]{1,0:T(1,128)} %reshape.28.nrow_ref, s32[1,384]{1,0:T(1,128)} %reshape.29.head_ref, s32[1,384]{1,0:T(1,128)} %reshape.30.rel_id_ref, ...), custom_call_target="tpu_custom_call" | custom-call | flops 30000001024 | bytes 7340032 | tf_op jit(solution)/shard_map/ranking_gradients/pallas_call | solution.py:453
  168.2 1.6 copy.12
  169.8 4.0 %copy.14 = f32[2048,400]{0,1:T(8,128)} copy(f32[2048,400]{0,1:T(8,128)} %bitcast.8) | data formatting | bytes 6553600

commit v3 on v2

v3 whole, which is shorter than its diff:
```python
import jax
import jax.numpy as jnp
from jax import lax
from jax.experimental import pallas as pl
from jax.experimental.pallas import tpu as pltpu
from jax.sharding import PartitionSpec as P

SPAN = 128
MAIN = 384
WIDE = 512
SLOTS = 16
CAP_T = 12
F32, BF16, I32 = jnp.float32, jnp.bfloat16, jnp.int32
MESH = pl.DeviceIdType.MESH
HIGHEST = lax.Precision.HIGHEST
NN = (((1,), (0,)), ((), ()))
NT = (((1,), (1,)), ((), ()))
TN = (((0,), (0,)), ((), ()))


def iota(shape, dim):
    return lax.broadcasted_iota(I32, shape, dim)


def parts(x, count):
    out = []
    for _ in range(count - 1):
        hi = x.astype(BF16)
        out.append(hi)
        x = x - hi.astype(F32)
    return out + [x.astype(BF16)]


def dot(a, b, dims):
    return lax.dot_general(a, b, dims, preferred_element_type=F32)


def dot_parts(onehot, values, dims=NN):
    total = dot(onehot, values[0], dims)
    for v in values[1:]:
        total = total + dot(onehot, v, dims)
    return total


def column(row):
    n = row.shape[1]
    return jnp.broadcast_to(row.astype(F32), (8, n)).T[:, 0:1].astype(I32)


def onehot(mask):
    return jnp.where(mask, 1.0, 0.0).astype(BF16)


def fold_matrix(rows, cols):
    l, m = iota((rows, cols), 0), iota((rows, cols), 1)
    return onehot((l & 15) == m)


def spread_matrix(rows, cols):
    m, l = iota((rows, cols), 0), iota((rows, cols), 1)
    return onehot((l & 15) == m)


DZ = (4, 5, 3, 6, 2, 7, 1, 0)
CHUNKS = 3


def id_column(ids, first):
    p = ids.shape[0]
    spread = jnp.broadcast_to(ids.astype(F32), (p, SLOTS, 128))
    own = iota((p, SLOTS, 128), 1) + first == iota((p, SLOTS, 128), 2)
    return jnp.sum(jnp.where(own, spread, 0.0), axis=2, keepdims=True).reshape(p * SLOTS, 1).astype(I32)


def kernel(
    towner_in, trow_in, nowner_in, nrow_in, head_in, rel_id_in, rel_in, et_in,
    out_ref, rel_out,
    towner_ref, trow_ref, nowner_ref, nrow_ref, head_ref, rel_id_ref, rel_ref, et_ref, hi_ref, mid_ref, lo_ref, oh_ref, ids_ref, line_ref, asked_ref, served_ref, fetched_ref, got_ref, negs_ref,
    head_emb, rel_rows, query_ref, gh_ref, gt_ref, gn_ref, gn_held, back_ref, recv_ref, vt_hi, vt_lo, held_ref, sums_ref,
    gr_ref, gr_recv, gr_sum, rel_recv,
    load_sem, ids_send, ids_recv, line_send, line_recv, serve_send, serve_recv, neg_send, neg_recv, gn_send, gn_recv,
    back_send, back_recv, gr_send, gr_got, ag_send, ag_recv, ring_send, ring_recv,
):
    peers = served_ref.shape[0]
    others = peers - 1
    n = negs_ref.shape[0]
    me, g = lax.axis_index("dom"), lax.axis_index("rel")
    edges, negs = head_ref.shape[0], nowner_ref.shape[1]
    quarter = negs // n
    lists = WIDE
    slots = peers * SLOTS
    width, rows = et_ref.shape
    tables = (hi_ref, mid_ref, lo_ref)
    z, y, core = lax.div(me, 8), lax.rem(lax.div(me, 2), 4), lax.rem(me, 2)
    spot = lax.rem(me, 8)
    z_plus = [lax.rem(z + d, 8) * 8 for d in DZ]
    z_minus = [lax.rem(z + 8 - d, 8) * 8 for d in DZ]

    def spot_plus(m):
        q = 7 - m
        return lax.rem(y + lax.div(q, 2), 4) * 2 + lax.rem(core + lax.rem(q, 2), 2)

    def spot_minus(m):
        q = 7 - m
        return lax.rem(y + 4 - lax.div(q, 2), 4) * 2 + lax.rem(core + lax.rem(q, 2), 2)

    def dom_copy(src, dst, send, recv, device):
        return pltpu.make_async_remote_copy(
            src, dst, send, recv, device_id={"dom": device}, device_id_type=MESH)

    def to_all(start, own):
        @pl.loop(0, 8)
        def _(m):
            for j in range(7):
                start(m * 8 + j, m, j)

            @pl.when(m < 7)
            def _():
                start(m * 8 + 7, m, 7)

        own()

    loads = [
        pltpu.make_async_copy(src, dst, load_sem.at[i])
        for i, (src, dst) in enumerate((
            (towner_in, towner_ref), (trow_in, trow_ref), (nowner_in, nowner_ref), (nrow_in, nrow_ref),
            (et_in, et_ref), (head_in, head_ref), (rel_id_in, rel_id_ref), (rel_in, rel_ref)))
    ]
    for load in loads:
        load.start()
    barrier = pltpu.get_barrier_semaphore()
    for j in range(7):
        pl.semaphore_signal(barrier, inc=1, device_id={"dom": z_plus[j] + spot}, device_id_type=MESH)
    for m in range(7):
        pl.semaphore_signal(barrier, inc=1, device_id={"dom": z * 8 + spot_plus(m)}, device_id_type=MESH)
    for k in range(1, n):
        pl.semaphore_signal(barrier, inc=1, device_id={"rel": lax.rem(g + k, n)}, device_id_type=MESH)

    for load in loads[0:4]:
        load.wait()

    def mine(row):
        return sum(jnp.where(g == q, row[:, quarter * q : quarter * (q + 1)], 0) for q in range(n))

    spare = jnp.zeros((1, lists - edges - quarter), I32)
    owner = jnp.concatenate([towner_ref[...], mine(nowner_ref[...]) + 64, spare + 255], axis=1)
    asked_rows = jnp.concatenate([trow_ref[...][None, :], mine(nrow_ref[...][None, :]), spare], axis=1)
    same = column(owner) == owner
    earlier = iota((lists, lists), 0) < iota((lists, lists), 1)
    position = jnp.sum(jnp.where(same & earlier, 1.0, 0.0), axis=0, keepdims=True).astype(I32)
    negative, valid = owner >= 64, owner < 128
    position = jnp.where(negative, position + CAP_T, position)
    owner = owner & 63
    dz = ((owner >> 3) - z + 8) & 7
    step_z = sum(jnp.where(dz == d, j, 0) for j, d in enumerate(DZ))
    dy, dc = (((owner >> 1) & 3) - y + 4) & 3, ((owner & 1) - core + 2) & 1
    slot = jnp.where(valid, ((7 - dy * 2 - dc) * 8 + step_z) * SLOTS + position, -1)
    left = jnp.where((iota((8, lists), 0) == step_z) & valid, (asked_rows + 1).astype(F32), 0.0)
    right = jnp.where(iota((128, lists), 0) == (owner & 7) * SLOTS + position, 1.0, 0.0)
    ids = lax.dot_general(left, right, NT, precision=HIGHEST, preferred_element_type=F32)
    ids_ref[...] = ((ids + 0.5).astype(I32) - 1)[:, None, :]

    pl.semaphore_wait(barrier, 14 + n - 1)
    for j in range(7):
        dom_copy(ids_ref.at[j], line_ref.at[j], ids_send, ids_recv, z_plus[j] + spot).start()
    pltpu.make_async_copy(ids_ref.at[7], line_ref.at[7], ids_recv).start()
    pltpu.make_async_copy(ids_ref, line_ref, ids_recv).wait()
    for m in range(7):
        dom_copy(line_ref, asked_ref.at[8 * m : 8 * m + 8], line_send, line_recv, z * 8 + spot_plus(m)).start()
    pltpu.make_async_copy(line_ref, asked_ref.at[56:64], line_recv).start()

    for load in loads[4:]:
        load.wait()

    @pl.loop(0, width // 16)
    def _(i):
        at = pl.multiple_of(i * 16, 16)
        for t, v in zip(tables, parts(et_ref[pl.ds(at, 16), :], 3), strict=True):
            t[pl.ds(at, 16), :] = v

    for t in tables:
        for k in range(1, 8):
            t[MAIN + 16 * k : MAIN + 16 * (k + 1), :] = t[MAIN : MAIN + 16, :]

    pltpu.make_async_copy(asked_ref, asked_ref, line_recv).wait()

    @pl.loop(0, 8)
    def _(m):
        at = pl.multiple_of(m * 8, 8)
        col = id_column(asked_ref[pl.ds(at, 8)], spot * SLOTS)
        hot = onehot(iota((8 * SLOTS, rows), 1) == col)
        oh_ref[pl.ds(pl.multiple_of(m * 8 * SLOTS, 8 * SLOTS), 8 * SLOTS), :] = hot
        got = dot_parts(hot, [t[...] for t in tables], NT)
        place = iota((8, SLOTS, 128), 1)
        lane = iota((8, SLOTS, 128), 2)
        rest = got[:, MAIN:].reshape(8, SLOTS, 128)
        rest = jnp.where((lane >> 4) == (place & 7), rest, 0.0)
        low = jnp.sum(jnp.where(place < 8, rest, 0.0), axis=1, keepdims=True)
        high = jnp.sum(jnp.where(place < 8, 0.0, rest), axis=1, keepdims=True)
        for k, part in enumerate((low, high, jnp.zeros_like(low))):
            main = got[:, 128 * k : 128 * (k + 1)].reshape(8, SLOTS, 128)
            served_ref[pl.ds(at, 8), :, 128 * k : 128 * (k + 1)] = jnp.where(place == SLOTS - 1, part, main)
        to = spot_minus(m)

        def start(i, j):
            dom_copy(served_ref.at[i], fetched_ref.at[i], serve_send, serve_recv.at[m], z_minus[j] + to).start()

        for j in range(7):
            start(m * 8 + j, j)

        @pl.when(m < 7)
        def _():
            start(m * 8 + 7, 7)

    pltpu.make_async_copy(served_ref.at[others], fetched_ref.at[others], serve_recv.at[7]).start()

    hot = onehot(iota((edges, rows), 1) == column(head_ref[...][None, :]))
    oh_ref[slots:, :] = hot
    got = dot_parts(hot, [t[...] for t in tables], NT)
    head_emb[:, 0:MAIN] = got[:, 0:MAIN]
    head_emb[:, MAIN:WIDE] = jnp.where(iota((edges, 128), 1) < width - MAIN, got[:, MAIN:WIDE], 0.0)
    groups = rel_ref.shape[0]
    hot = onehot(iota((edges, groups), 1) == column(rel_id_ref[...][None, :]))
    rel_rows[:, 0:width] = dot_parts(hot, parts(rel_ref[...], 3))
    rel_rows[:, width:WIDE] = jnp.zeros((edges, WIDE - width), F32)
    query_ref[...] = head_emb[...] * rel_rows[...]

    slot_col = column(slot)
    fold = fold_matrix(256, 128)
    got_ref[...] = jnp.zeros_like(got_ref)

    @pl.loop(0, 4)
    def _(b):
        at = pl.ds(pl.multiple_of(b * 16, 16), 16)
        for k in range(2):
            half = pl.ds(pl.multiple_of(b * 16, 16) + 8 * k, 8)
            pltpu.make_async_copy(served_ref.at[half], fetched_ref.at[half], serve_recv.at[2 * b + k]).wait()
        hot = onehot(iota((lists, 16 * SLOTS), 1) + b * (16 * SLOTS) == slot_col)
        got_ref[:, 0:MAIN] += dot_parts(hot, parts(fetched_ref[at].reshape(16 * SLOTS, MAIN), 3))

    packed = parts(fetched_ref[:, SLOTS - 1, 0:256], 3)

    def remainders(at):
        where = slot_col[at]
        count = where.shape[0]
        rest = dot_parts(onehot(iota((count, peers), 1) == (where >> 4)), packed)
        rest = jnp.where((iota((count, 256), 1) >> 4) == (where & 15), rest, 0.0)
        return sum(dot(p, fold, NN) for p in parts(rest, 3))

    own = slice(edges, edges + quarter)
    negs_ref[g, :, 0:MAIN] = got_ref[own, 0:MAIN]
    negs_ref[g, :, MAIN:WIDE] = remainders(own)

    def rel_copy(src, dst, send, recv, k):
        return pltpu.make_async_remote_copy(
            src, dst, send, recv, device_id={"rel": lax.rem(g + k, n)}, device_id_type=MESH)

    copies = [rel_copy(negs_ref.at[g], negs_ref.at[g], neg_send.at[k - 1], neg_recv.at[k - 1], k) for k in range(1, n)]
    for copy in copies:
        copy.start()
    got_ref[0:edges, MAIN:WIDE] = remainders(slice(0, edges))
    positive = jnp.sum(query_ref[...] * got_ref[0:edges, :], axis=1, keepdims=True)
    for copy in copies:
        copy.wait_recv()
    sent = list(copies)

    def neg_rows(c):
        return negs_ref[...].reshape(negs, WIDE)[c * SPAN : (c + 1) * SPAN]

    coefs = []
    for c in range(edges // SPAN):
        at = slice(c * SPAN, (c + 1) * SPAN)
        queries = query_ref[at]
        scores = lax.dot_general(queries, neg_rows(c), NT, precision=HIGHEST, preferred_element_type=F32)
        row_max = jnp.maximum(positive[at], jnp.max(scores, axis=1, keepdims=True))
        pos_exp = jnp.exp(positive[at] - row_max)
        neg_exp = jnp.exp(scores - row_max)
        total = pos_exp + jnp.sum(neg_exp, axis=1, keepdims=True)
        pos_coef = pos_exp / total - 1.0
        neg_coef = neg_exp / total
        coefs.append((pos_coef, neg_coef))
        gt_ref[at] = pos_coef * queries
        grad_neg = lax.dot_general(neg_coef.T, queries, NN, precision=HIGHEST, preferred_element_type=F32)
        first = c * SPAN
        while first < (c + 1) * SPAN:
            q, inside = divmod(first, quarter)
            count = min(quarter - inside, (c + 1) * SPAN - first)
            gn_ref[q, inside : inside + count] = grad_neg[first - c * SPAN : first - c * SPAN + count]
            first += count

    copies = [
        rel_copy(gn_ref.at[lax.rem(g + k, n)], gn_held.at[k - 1], gn_send.at[k - 1], gn_recv.at[k - 1], k) for k in range(1, n)
    ]
    for copy in copies:
        copy.start()

    def send_back(k, part, at):
        def start(i, m, j):
            dom_copy(
                back_ref.at[k, i, at], recv_ref.at[k, i, at], back_send, back_recv.at[part], z_plus[j] + spot_plus(m)).start()

        def own():
            pltpu.make_async_copy(back_ref.at[k, others, at], recv_ref.at[k, others, at], back_recv.at[part]).start()

        to_all(start, own)

    hot = onehot(iota((slots, edges), 0) == slot[:, 0:edges])
    low, high, all_rows = pl.ds(0, 8), pl.ds(8, 8), pl.ds(0, SLOTS)
    for k in range(CHUNKS):
        back_ref[k] = dot_parts(hot, parts(gt_ref[:, 128 * k : 128 * (k + 1)], 2)).reshape(peers, SLOTS, 128)
        if k == 0:
            send_back(0, 0, low)

    spread = spread_matrix(128, 256)

    def remainders_back(values, at):
        count = values.shape[0]
        rest = sum(dot(p, spread, NN) for p in parts(values, 2))
        rest = jnp.where((iota((count, 256), 1) >> 4) == (slot_col[at] & 15), rest, 0.0)
        return dot_parts(onehot(iota((peers, count), 0) == (slot[:, at] >> 4)), parts(rest, 2))

    rest = remainders_back(gt_ref[:, MAIN:WIDE], slice(0, edges))
    for copy in copies:
        copy.wait_recv()
    sent += copies
    grad_neg = gn_ref[g] + gn_held[0] + gn_held[1] + gn_held[2]
    rest = rest + remainders_back(grad_neg[:, MAIN:WIDE], own)
    line = iota((peers * 8, quarter), 0)
    hot = onehot((line >> 3) * SLOTS + 8 + (line & 7) == slot[:, own])
    last = iota((peers, 8, 128), 1) == 7
    for k in range(CHUNKS):
        more = dot_parts(hot, parts(grad_neg[:, 128 * k : 128 * (k + 1)], 2)).reshape(peers, 8, 128)
        more = back_ref[k, :, 8:SLOTS, :] + more
        if k < 2:
            more = jnp.where(last, rest[:, 128 * k : 128 * (k + 1)][:, None, :], more)
        back_ref[k, :, 8:SLOTS, :] = more
        send_back(k, k + 1, high if k == 0 else all_rows)

    gr_parts = []
    for c in range(edges // SPAN):
        at = slice(c * SPAN, (c + 1) * SPAN)
        pos_coef, neg_coef = coefs[c]
        grad_query = pos_coef * got_ref[at] + lax.dot_general(
            neg_coef, neg_rows(c), NN, precision=HIGHEST, preferred_element_type=F32)
        gh_ref[at] = grad_query * rel_rows[at]
        hot = onehot(iota((groups, SPAN), 0) == rel_id_ref[at][None, :])
        gr_parts.append(dot_parts(hot, parts(grad_query * head_emb[at], 3)))
    gr_ref[...] = sum(gr_parts)[:, None, :]

    def start_rel(i, m, j):
        to = z_plus[j] + spot_plus(m)
        dom_copy(gr_ref.at[to], gr_recv.at[i], gr_send, gr_got, to).start()

    to_all(start_rel, lambda: pltpu.make_async_copy(gr_ref.at[me], gr_recv.at[others], gr_got).start())

    slab_ref = et_ref
    piece = rows // n
    right_hand, left_hand, far = lax.rem(g + 1, n), lax.rem(g + 3, n), lax.rem(g + 2, n)
    first_row = [128 * k for k in range(CHUNKS)]
    height = [128] * (CHUNKS - 1) + [width - 128 * (CHUNKS - 1)]

    def cols(j):
        return pl.ds(pl.multiple_of(j * piece, piece), piece)

    ring = {}
    to_of, back_of = (right_hand, left_hand), (left_hand, right_hand)

    def half(k, way, mine):
        h = height[k] // 2
        low = (way == 0) == mine
        return slice(first_row[k], first_row[k] + h) if low else slice(first_row[k] + h, first_row[k] + 2 * h)

    def send(k, way, step, src, dst):
        copy = pltpu.make_async_remote_copy(
            src, dst, ring_send.at[k, way, step], ring_recv.at[k, way, step],
            device_id={"rel": to_of[way]}, device_id_type=MESH)
        copy.start()
        ring[k, way, step] = copy

    def arrived(k, part, at):
        pltpu.make_async_copy(back_ref.at[k, :, at], recv_ref.at[k, :, at], back_recv.at[part]).wait()

    def scatter(k):
        if k == 0:
            arrived(0, 0, low)
            arrived(0, 1, high)
        else:
            arrived(k, k + 1, all_rows)
        values = [recv_ref[k].reshape(slots, 128).T, gh_ref[:, 128 * k : 128 * (k + 1)].T]
        vt = jnp.concatenate(values, axis=1)
        if k == CHUNKS - 1:
            rest = jnp.concatenate([recv_ref[0, :, SLOTS - 1, :], recv_ref[1, :, SLOTS - 1, :]], axis=1)
            rest = jnp.broadcast_to(rest[:, None, :], (peers, SLOTS, 256))
            own = (iota((peers, SLOTS, 256), 2) >> 4) == iota((peers, SLOTS, 256), 1)
            rest = jnp.where(own, rest, 0.0).reshape(slots, 256)
            rest = sum(dot(p, fold, NN) for p in parts(rest, 2))
            more = jnp.concatenate([rest.T[0:16], gh_ref[:, MAIN:WIDE].T[0:16]], axis=1)
            vt = jnp.concatenate([vt, more], axis=0)
        h = height[k]
        vt_hi[0:h], vt_lo[0:h] = parts(vt, 2)

        @pl.loop(0, n)
        def _(j):
            at = cols(j)
            slab_ref[first_row[k] : first_row[k] + h, at] = dot(vt_hi[0:h], oh_ref[:, at], NN) + dot(
                vt_lo[0:h], oh_ref[:, at], NN)

    def begin(k):
        h = height[k] // 2
        for way in range(2):
            send(k, way, 0, slab_ref.at[half(k, way, True), cols(far)], held_ref.at[k, way, 0, 0:h])
        for way in range(2):
            send(k, way, 1, slab_ref.at[half(k, way, False), cols(to_of[way])], held_ref.at[k, way, 1, 0:h])

    def add(k):
        h = height[k] // 2
        for way in range(2):
            ring[k, way, 0].wait_recv()
            sums_ref[k, way, 0:h] = slab_ref[half(k, way, True), cols(to_of[way])] + held_ref[k, way, 0, 0:h]
            send(k, way, 2, sums_ref.at[k, way, 0:h], held_ref.at[k, way, 2, 0:h])

    def share(k):
        h = height[k] // 2
        for way in range(2):
            ring[k, way, 1].wait_recv()
            ring[k, way, 2].wait_recv()
        for way in range(2):
            at = half(k, way, True)
            out_ref[at, cols(g)] = slab_ref[at, cols(g)] + held_ref[k, way, 2, 0:h] + held_ref[k, 1 - way, 1, 0:h]
        for step, mine_too in ((3, True), (4, False)):
            for way in range(2):
                at = half(k, way, mine_too)
                send(k, way, step, out_ref.at[at, cols(g)], out_ref.at[at, cols(g)])

    def forward(k):
        for way in range(2):
            ring[k, way, 3].wait_recv()
            at = half(k, way, True)
            send(k, way, 5, out_ref.at[at, cols(back_of[way])], out_ref.at[at, cols(back_of[way])])

    scatter(0)
    begin(0)
    pltpu.make_async_copy(gr_ref, gr_recv, gr_got).wait()
    gr_sum[0] = jnp.sum(gr_recv[...], axis=0)

    def start_sum(i, m, j):
        dom_copy(gr_sum.at[0], rel_recv.at[me], ag_send, ag_recv, z_plus[j] + spot_plus(m)).start()

    to_all(start_sum, lambda: pltpu.make_async_copy(gr_sum.at[0], rel_recv.at[me], ag_recv).start())
    add(0)
    share(0)
    scatter(1)
    begin(1)
    forward(0)
    add(1)
    share(1)
    scatter(2)
    begin(2)
    forward(1)
    add(2)
    share(2)
    pltpu.make_async_copy(gr_ref, rel_recv, ag_recv).wait()
    rel_out[...] = rel_recv[:, 0, :][:, 0:width]
    forward(2)

    first = pl.ds(0, others)
    seven = pl.ds(0, 7)
    pltpu.make_async_copy(ids_ref.at[seven], ids_ref.at[seven], ids_send).wait()
    pltpu.make_async_copy(asked_ref.at[0:56], asked_ref.at[0:56], line_send).wait()
    pltpu.make_async_copy(served_ref.at[first], served_ref.at[first], serve_send).wait()
    pltpu.make_async_copy(gr_ref.at[first], gr_ref.at[first], gr_send).wait()
    pltpu.make_async_copy(gr_ref.at[first], gr_ref.at[first], ag_send).wait()
    for k in range(CHUNKS):
        pltpu.make_async_copy(back_ref.at[k, first], back_ref.at[k, first], back_send).wait()
    for copy in [*sent, *ring.values()]:
        copy.wait_send()
    for k in range(CHUNKS):
        for way in range(2):
            ring[k, way, 4].wait_recv()
            ring[k, way, 5].wait_recv()


def body(embeddings, rel_weight, head_row, rel_id, tail_owner, tail_row, neg_owner, neg_row):
    peers, n = lax.axis_size("dom"), lax.axis_size("rel")
    rows, width = embeddings.shape
    edges, negs = head_row.shape[0], neg_row.shape[0]
    groups = rel_weight.shape[0]
    quarter = negs // n
    lists = WIDE
    slots = peers * SLOTS
    tall = (width - 128 * (CHUNKS - 1)) // 2
    V, DMA = pltpu.VMEM, pltpu.SemaphoreType.DMA
    vmem, in_hbm = pl.BlockSpec(memory_space=pltpu.VMEM), pl.BlockSpec(memory_space=pltpu.HBM)
    scratch = [
        V((1, edges), I32), V((edges,), I32), V((1, negs), I32), V((negs,), I32), V((edges,), I32), V((edges,), I32),
        V((groups, width), F32), V((width, rows), F32), V((WIDE, rows), BF16), V((WIDE, rows), BF16), V((WIDE, rows), BF16),
        V((slots + edges, rows), BF16), V((8, 1, 128), I32), V((8, 1, 128), I32), V((peers, 1, 128), I32),
        V((peers, SLOTS, MAIN), F32), V((peers, SLOTS, MAIN), F32), V((lists, WIDE), F32), V((n, quarter, WIDE), F32),
        V((edges, WIDE), F32), V((edges, WIDE), F32), V((edges, WIDE), F32), V((edges, WIDE), F32), V((edges, WIDE), F32),
        V((n, quarter, WIDE), F32), V((n - 1, quarter, WIDE), F32),
        V((CHUNKS, peers, SLOTS, 128), F32), V((CHUNKS, peers, SLOTS, 128), F32),
        V((2 * tall, slots + edges), BF16), V((2 * tall, slots + edges), BF16),
        V((CHUNKS, 2, 3, tall, rows // n), F32), V((CHUNKS, 2, tall, rows // n), F32),
        V((groups, 1, WIDE), F32), V((peers, 1, WIDE), F32), V((1, 1, WIDE), F32), V((groups, 1, WIDE), F32),
        DMA((8,)), DMA(()), DMA(()), DMA(()), DMA(()), DMA(()), DMA((8,)), DMA((n - 1,)), DMA((n - 1,)), DMA((n - 1,)), DMA((n - 1,)),
        DMA(()), DMA((CHUNKS + 1,)), DMA(()), DMA(()), DMA(()), DMA(()), DMA((CHUNKS, 2, 6)), DMA((CHUNKS, 2, 6)),
    ]
    total, relation = pl.pallas_call(
        kernel,
        out_shape=(jax.ShapeDtypeStruct((width, rows), F32), jax.ShapeDtypeStruct((groups, width), F32)),
        in_specs=[in_hbm] * 8,
        out_specs=(vmem, vmem),
        scratch_shapes=scratch,
        compiler_params=pltpu.CompilerParams(collective_id=0, has_side_effects=True, vmem_limit_bytes=48 << 20),
        cost_estimate=pl.CostEstimate(flops=int(3e10), bytes_accessed=7 << 20, transcendentals=0),
        name="ranking_gradients",
    )(
        tail_owner.reshape(1, edges), tail_row, neg_owner.reshape(1, negs), neg_row, head_row, rel_id, rel_weight, embeddings.T)
    return (total.T, relation)


def solution(mesh):
    return jax.shard_map(
        body,
        mesh=mesh,
        in_specs=(
            P("dom", None),
            P("rel", None),
            P(("dom", "rel")),
            P(("dom", "rel")),
            P(("dom", "rel"), None),
            P(("dom", "rel")),
            P("dom", None),
            P("dom"),
        ),
        out_specs=(P("dom", None), P("rel", None)),
        check_vma=False,
    )
```

time: 174 us -> 177 us (1.017)
  Pallas kernels: 163 us -> 168 us
  local copies, waits for them, and re-layouts: 10.6 us -> 7.35 us
    pallas_call x1, Pallas kernels: 163 us -> 168 us  [body(): pl.pallas_call(kernel, out_shape=(jax.ShapeDtypeStruct((width, rows), F32...]
    reshape x4 -> x0, local copies, waits for them, and re-layouts: 5.03 us -> none  [the longest x1 1.27 us: body(): rel_id.reshape(1, edges)]
    unnamed x2 -> x16, local copies, waits for them, and re-layouts: 5.58 us -> 7.35 us
where the time goes in v3:
time: 177 us; the launch traced here: 176 us
  Pallas kernels  168 us (95%)
  local copies, waits for them, and re-layouts  7.35 us (4%)
    pallas_call x1, Pallas kernels, body(): pl.pallas_call(kernel, out_shape=(jax.ShapeDtypeStruct((width, rows), F32...  168 us
    unnamed x16, local copies, waits for them, and re-layouts  7.35 us

profile of v3, /device:TPU:2, one launch (start us, length us, event | category | flops | bytes accessed | tf_op | source)
XLA Modules:
  0.0 176.0 jit_solution(14279706389805404828)
XLA Ops:
  0.6 0.0 copy-start
  0.6 0.9 copy-done
  1.5 0.0 copy-start.1
  1.5 0.7 copy-done.1
  2.2 0.0 copy-start.2
  2.2 0.7 copy-done.2
  2.9 0.0 copy-start.3
  2.9 0.7 copy-done.3
  3.6 0.0 copy-start.4
  3.6 0.7 copy-done.4
  4.3 0.0 copy-start.5
  4.3 0.7 copy-done.5
  4.9 0.0 copy-start.6
  4.9 0.7 copy-done.6
  5.6 168.0 %ranking_gradients.1 = (f32[400,2048]{1,0:T(8,128)S(1)}, f32[64,400]{1,0:T(8,128)S(1)}) custom-call(s32[1,384]{1,0:T(1,128)S(1)} %bitcast.5, s32[384]{0:T(512)S(1)} %copy-done.1, s32[1,384]{1,0:T(1,128)S(1)} %bitcast.6, s32[384]{0:T(512)S(1)} %copy-done.2, s32[384]{0:T(512)S(1)} %copy-done.3, s32[384]{0:T(512)S(1)} %copy-done.4, f32[64,400]{1,0:T(8,128)S(1)} %copy-done, ...), custom_call_target="tpu_custom_call" | custom-call | flops 30000001024 | bytes 7340032 | tf_op jit(solution)/shard_map/ranking_gradients/pallas_call | solution.py:508
  173.6 1.7 copy.12
  175.3 0.7 copy.13
Async XLA Ops:
  0.6 0.9 copy-start
  1.5 0.7 copy-start.1
  2.2 0.7 copy-start.2
  2.9 0.7 copy-start.3
  3.6 0.7 copy-start.4
  4.3 0.7 copy-start.5
  4.9 0.7 copy-start.6

commit v4 on v3

--- a/solution.py
+++ b/solution.py
@@ -73,9 +73,9 @@
 
 
 def kernel(
-    towner_in, trow_in, nowner_in, nrow_in, head_in, rel_id_in, rel_in, et_in,
+    lists_ref, rel_in, et_in,
     out_ref, rel_out,
-    towner_ref, trow_ref, nowner_ref, nrow_ref, head_ref, rel_id_ref, rel_ref, et_ref, hi_ref, mid_ref, lo_ref, oh_ref, ids_ref, line_ref, asked_ref, served_ref, fetched_ref, got_ref, negs_ref,
+    rel_ref, et_ref, hi_ref, mid_ref, lo_ref, oh_ref, ids_ref, line_ref, asked_ref, served_ref, fetched_ref, got_ref, negs_ref,
     head_emb, rel_rows, query_ref, gh_ref, gt_ref, gn_ref, gn_held, back_ref, recv_ref, vt_hi, vt_lo, held_ref, sums_ref,
     gr_ref, gr_recv, gr_sum, rel_recv,
     load_sem, ids_send, ids_recv, line_send, line_recv, serve_send, serve_recv, neg_send, neg_recv, gn_send, gn_recv,
@@ -85,7 +85,8 @@
     others = peers - 1
     n = negs_ref.shape[0]
     me, g = lax.axis_index("dom"), lax.axis_index("rel")
-    edges, negs = head_ref.shape[0], nowner_ref.shape[1]
+    edges = head_emb.shape[0]
+    negs = (lists_ref.shape[1] - 4 * edges) // 2
     quarter = negs // n
     lists = WIDE
     slots = peers * SLOTS
@@ -120,12 +121,7 @@
 
         own()
 
-    loads = [
-        pltpu.make_async_copy(src, dst, load_sem.at[i])
-        for i, (src, dst) in enumerate((
-            (towner_in, towner_ref), (trow_in, trow_ref), (nowner_in, nowner_ref), (nrow_in, nrow_ref),
-            (et_in, et_ref), (head_in, head_ref), (rel_id_in, rel_id_ref), (rel_in, rel_ref)))
-    ]
+    loads = [pltpu.make_async_copy(et_in, et_ref, load_sem.at[0]), pltpu.make_async_copy(rel_in, rel_ref, load_sem.at[1])]
     for load in loads:
         load.start()
     barrier = pltpu.get_barrier_semaphore()
@@ -136,15 +132,15 @@
     for k in range(1, n):
         pl.semaphore_signal(barrier, inc=1, device_id={"rel": lax.rem(g + k, n)}, device_id_type=MESH)
 
-    for load in loads[0:4]:
-        load.wait()
+    tail_owner, tail_row, head_row, rel_id = (lists_ref[:, edges * k : edges * (k + 1)] for k in range(4))
+    neg_owner, neg_row = (lists_ref[:, 4 * edges + negs * k : 4 * edges + negs * (k + 1)] for k in range(2))
 
     def mine(row):
         return sum(jnp.where(g == q, row[:, quarter * q : quarter * (q + 1)], 0) for q in range(n))
 
     spare = jnp.zeros((1, lists - edges - quarter), I32)
-    owner = jnp.concatenate([towner_ref[...], mine(nowner_ref[...]) + 64, spare + 255], axis=1)
-    asked_rows = jnp.concatenate([trow_ref[...][None, :], mine(nrow_ref[...][None, :]), spare], axis=1)
+    owner = jnp.concatenate([tail_owner, mine(neg_owner) + 64, spare + 255], axis=1)
+    asked_rows = jnp.concatenate([tail_row, mine(neg_row), spare], axis=1)
     same = column(owner) == owner
     earlier = iota((lists, lists), 0) < iota((lists, lists), 1)
     position = jnp.sum(jnp.where(same & earlier, 1.0, 0.0), axis=0, keepdims=True).astype(I32)
@@ -169,7 +165,7 @@
         dom_copy(line_ref, asked_ref.at[8 * m : 8 * m + 8], line_send, line_recv, z * 8 + spot_plus(m)).start()
     pltpu.make_async_copy(line_ref, asked_ref.at[56:64], line_recv).start()
 
-    for load in loads[4:]:
+    for load in loads:
         load.wait()
 
     @pl.loop(0, width // 16)
@@ -214,13 +210,13 @@
 
     pltpu.make_async_copy(served_ref.at[others], fetched_ref.at[others], serve_recv.at[7]).start()
 
-    hot = onehot(iota((edges, rows), 1) == column(head_ref[...][None, :]))
+    hot = onehot(iota((edges, rows), 1) == column(head_row))
     oh_ref[slots:, :] = hot
     got = dot_parts(hot, [t[...] for t in tables], NT)
     head_emb[:, 0:MAIN] = got[:, 0:MAIN]
     head_emb[:, MAIN:WIDE] = jnp.where(iota((edges, 128), 1) < width - MAIN, got[:, MAIN:WIDE], 0.0)
     groups = rel_ref.shape[0]
-    hot = onehot(iota((edges, groups), 1) == column(rel_id_ref[...][None, :]))
+    hot = onehot(iota((edges, groups), 1) == column(rel_id))
     rel_rows[:, 0:width] = dot_parts(hot, parts(rel_ref[...], 3))
     rel_rows[:, width:WIDE] = jnp.zeros((edges, WIDE - width), F32)
     query_ref[...] = head_emb[...] * rel_rows[...]
@@ -343,7 +339,7 @@
         grad_query = pos_coef * got_ref[at] + lax.dot_general(
             neg_coef, neg_rows(c), NN, precision=HIGHEST, preferred_element_type=F32)
         gh_ref[at] = grad_query * rel_rows[at]
-        hot = onehot(iota((groups, SPAN), 0) == rel_id_ref[at][None, :])
+        hot = onehot(iota((groups, SPAN), 0) == rel_id[:, at])
         gr_parts.append(dot_parts(hot, parts(grad_query * head_emb[at], 3)))
     gr_ref[...] = sum(gr_parts)[:, None, :]
 
@@ -440,13 +436,6 @@
 
     scatter(0)
     begin(0)
-    pltpu.make_async_copy(gr_ref, gr_recv, gr_got).wait()
-    gr_sum[0] = jnp.sum(gr_recv[...], axis=0)
-
-    def start_sum(i, m, j):
-        dom_copy(gr_sum.at[0], rel_recv.at[me], ag_send, ag_recv, z_plus[j] + spot_plus(m)).start()
-
-    to_all(start_sum, lambda: pltpu.make_async_copy(gr_sum.at[0], rel_recv.at[me], ag_recv).start())
     add(0)
     share(0)
     scatter(1)
@@ -457,6 +446,13 @@
     scatter(2)
     begin(2)
     forward(1)
+    pltpu.make_async_copy(gr_ref, gr_recv, gr_got).wait()
+    gr_sum[0] = jnp.sum(gr_recv[...], axis=0)
+
+    def start_sum(i, m, j):
+        dom_copy(gr_sum.at[0], rel_recv.at[me], ag_send, ag_recv, z_plus[j] + spot_plus(m)).start()
+
+    to_all(start_sum, lambda: pltpu.make_async_copy(gr_sum.at[0], rel_recv.at[me], ag_recv).start())
     add(2)
     share(2)
     pltpu.make_async_copy(gr_ref, rel_recv, ag_recv).wait()
@@ -489,10 +485,13 @@
     lists = WIDE
     slots = peers * SLOTS
     tall = (width - 128 * (CHUNKS - 1)) // 2
+    lists_of = [a.reshape(1, a.shape[0]) for a in (tail_owner, tail_row, head_row, rel_id, neg_owner, neg_row)]
+    ends = [sum(a.shape[1] for a in lists_of[: k + 1]) for k in range(len(lists_of))]
+    joined = sum(
+        jnp.pad(a, ((0, 0), (end - a.shape[1], ends[-1] - end))) for a, end in zip(lists_of, ends, strict=True))
     V, DMA = pltpu.VMEM, pltpu.SemaphoreType.DMA
     vmem, in_hbm = pl.BlockSpec(memory_space=pltpu.VMEM), pl.BlockSpec(memory_space=pltpu.HBM)
     scratch = [
-        V((1, edges), I32), V((edges,), I32), V((1, negs), I32), V((negs,), I32), V((edges,), I32), V((edges,), I32),
         V((groups, width), F32), V((width, rows), F32), V((WIDE, rows), BF16), V((WIDE, rows), BF16), V((WIDE, rows), BF16),
         V((slots + edges, rows), BF16), V((8, 1, 128), I32), V((8, 1, 128), I32), V((peers, 1, 128), I32),
         V((peers, SLOTS, MAIN), F32), V((peers, SLOTS, MAIN), F32), V((lists, WIDE), F32), V((n, quarter, WIDE), F32),
@@ -502,20 +501,19 @@
         V((2 * tall, slots + edges), BF16), V((2 * tall, slots + edges), BF16),
         V((CHUNKS, 2, 3, tall, rows // n), F32), V((CHUNKS, 2, tall, rows // n), F32),
         V((groups, 1, WIDE), F32), V((peers, 1, WIDE), F32), V((1, 1, WIDE), F32), V((groups, 1, WIDE), F32),
-        DMA((8,)), DMA(()), DMA(()), DMA(()), DMA(()), DMA(()), DMA((8,)), DMA((n - 1,)), DMA((n - 1,)), DMA((n - 1,)), DMA((n - 1,)),
+        DMA((2,)), DMA(()), DMA(()), DMA(()), DMA(()), DMA(()), DMA((8,)), DMA((n - 1,)), DMA((n - 1,)), DMA((n - 1,)), DMA((n - 1,)),
         DMA(()), DMA((CHUNKS + 1,)), DMA(()), DMA(()), DMA(()), DMA(()), DMA((CHUNKS, 2, 6)), DMA((CHUNKS, 2, 6)),
     ]
     total, relation = pl.pallas_call(
         kernel,
         out_shape=(jax.ShapeDtypeStruct((width, rows), F32), jax.ShapeDtypeStruct((groups, width), F32)),
-        in_specs=[in_hbm] * 8,
+        in_specs=[vmem, in_hbm, in_hbm],
         out_specs=(vmem, vmem),
         scratch_shapes=scratch,
         compiler_params=pltpu.CompilerParams(collective_id=0, has_side_effects=True, vmem_limit_bytes=48 << 20),
         cost_estimate=pl.CostEstimate(flops=int(3e10), bytes_accessed=7 << 20, transcendentals=0),
         name="ranking_gradients",
-    )(
-        tail_owner.reshape(1, edges), tail_row, neg_owner.reshape(1, negs), neg_row, head_row, rel_id, rel_weight, embeddings.T)
+    )(joined, rel_weight, embeddings.T)
     return (total.T, relation)
 
 

time: 177 us -> 158 us (0.89)
  Pallas kernels: 168 us -> 151 us
    pallas_call x1, Pallas kernels: 168 us -> 151 us  [body(): pl.pallas_call(kernel, out_shape=(jax.ShapeDtypeStruct((width, rows), F32...]
    unnamed x16 -> x4, local copies, waits for them, and re-layouts: 7.35 us -> 3.27 us
    reshape x0 -> x4, local copies, waits for them, and re-layouts: none -> 2.73 us  [body(): a.reshape(1, a.shape[0])]
where the time goes in v4:
time: 158 us
  Pallas kernels  151 us (96%)
  local copies, waits for them, and re-layouts  6 us (4%)
    pallas_call x1, Pallas kernels, body(): pl.pallas_call(kernel, out_shape=(jax.ShapeDtypeStruct((width, rows), F32...  151 us
    unnamed x4, local copies, waits for them, and re-layouts  3.27 us

profile of v4, /device:TPU:2, one launch (start us, length us, event | category | flops | bytes accessed | tf_op | source)
XLA Modules:
  0.0 157.9 jit_solution(5130206920313998764)
XLA Ops:
  0.6 0.7 reshape.24
  1.3 0.7 reshape.25
  2.0 0.7 reshape.23
  2.7 0.7 reshape.27
  3.4 0.7 pad_add_fusion.lists_ref
  4.1 0.0 copy-start
  4.1 0.9 copy-done
  5.0 150.6 %ranking_gradients.1 = (f32[400,2048]{1,0:T(8,128)S(1)}, f32[64,400]{1,0:T(8,128)S(1)}) custom-call(s32[1,2304]{1,0:T(1,128)S(1)} %pad_add_fusion.lists_ref, f32[64,400]{1,0:T(8,128)S(1)} %copy-done, f32[400,2048]{1,0:T(8,128)} %bitcast.7), custom_call_target="tpu_custom_call" | custom-call | flops 30000001024 | bytes 7340032 | tf_op jit(solution)/shard_map/ranking_gradients/pallas_call | solution.py:507
  155.5 1.7 %copy.12 = f32[2048,400]{0,1:T(8,128)} copy(f32[2048,400]{0,1:T(8,128)S(1)} %bitcast.4) | data formatting | bytes 6553600
  157.3 0.7 copy.13
Async XLA Ops:
  4.1 0.9 copy-start

commit v5 on v4

--- a/solution.py
+++ b/solution.py
@@ -73,12 +73,12 @@
 
 
 def kernel(
-    lists_ref, rel_in, et_in,
+    lists_ref, towner_ref, nowner_ref, rel_in, et_in,
     out_ref, rel_out,
     rel_ref, et_ref, hi_ref, mid_ref, lo_ref, oh_ref, ids_ref, line_ref, asked_ref, served_ref, fetched_ref, got_ref, negs_ref,
-    head_emb, rel_rows, query_ref, gh_ref, gt_ref, gn_ref, gn_held, back_ref, recv_ref, vt_hi, vt_lo, held_ref, sums_ref,
+    head_emb, rel_rows, query_ref, gh_ref, gt_ref, gn_ref, gn_held, gn_sums, back_ref, recv_ref, vt_hi, vt_lo, held_ref, sums_ref,
     gr_ref, gr_recv, gr_sum, rel_recv,
-    load_sem, ids_send, ids_recv, line_send, line_recv, serve_send, serve_recv, neg_send, neg_recv, gn_send, gn_recv,
+    load_sem, ids_send, ids_recv, line_send, line_recv, serve_send, high_recv, serve_recv, neg_send, neg_recv, gn_send, gn_recv,
     back_send, back_recv, gr_send, gr_got, ag_send, ag_recv, ring_send, ring_recv,
 ):
     peers = served_ref.shape[0]
@@ -86,7 +86,7 @@
     n = negs_ref.shape[0]
     me, g = lax.axis_index("dom"), lax.axis_index("rel")
     edges = head_emb.shape[0]
-    negs = (lists_ref.shape[1] - 4 * edges) // 2
+    negs = nowner_ref.shape[1]
     quarter = negs // n
     lists = WIDE
     slots = peers * SLOTS
@@ -108,6 +108,8 @@
     def dom_copy(src, dst, send, recv, device):
         return pltpu.make_async_remote_copy(
             src, dst, send, recv, device_id={"dom": device}, device_id_type=MESH)
+
+    low, high, all_rows = pl.ds(0, 8), pl.ds(8, 8), pl.ds(0, SLOTS)
 
     def to_all(start, own):
         @pl.loop(0, 8)
@@ -132,14 +134,14 @@
     for k in range(1, n):
         pl.semaphore_signal(barrier, inc=1, device_id={"rel": lax.rem(g + k, n)}, device_id_type=MESH)
 
-    tail_owner, tail_row, head_row, rel_id = (lists_ref[:, edges * k : edges * (k + 1)] for k in range(4))
-    neg_owner, neg_row = (lists_ref[:, 4 * edges + negs * k : 4 * edges + negs * (k + 1)] for k in range(2))
+    tail_row, head_row, rel_id = (lists_ref[:, edges * k : edges * (k + 1)] for k in range(3))
+    neg_row = lists_ref[:, 3 * edges : 3 * edges + negs]
 
     def mine(row):
         return sum(jnp.where(g == q, row[:, quarter * q : quarter * (q + 1)], 0) for q in range(n))
 
     spare = jnp.zeros((1, lists - edges - quarter), I32)
-    owner = jnp.concatenate([tail_owner, mine(neg_owner) + 64, spare + 255], axis=1)
+    owner = jnp.concatenate([towner_ref[...], mine(nowner_ref[...]) + 64, spare + 255], axis=1)
     asked_rows = jnp.concatenate([tail_row, mine(neg_row), spare], axis=1)
     same = column(owner) == owner
     earlier = iota((lists, lists), 0) < iota((lists, lists), 1)
@@ -191,15 +193,15 @@
         lane = iota((8, SLOTS, 128), 2)
         rest = got[:, MAIN:].reshape(8, SLOTS, 128)
         rest = jnp.where((lane >> 4) == (place & 7), rest, 0.0)
-        low = jnp.sum(jnp.where(place < 8, rest, 0.0), axis=1, keepdims=True)
-        high = jnp.sum(jnp.where(place < 8, 0.0, rest), axis=1, keepdims=True)
-        for k, part in enumerate((low, high, jnp.zeros_like(low))):
+        one = jnp.sum(jnp.where(place < 8, rest, 0.0), axis=1, keepdims=True)
+        two = jnp.sum(jnp.where(place < 8, 0.0, rest), axis=1, keepdims=True)
+        for k, part in enumerate((one, two, jnp.zeros_like(one))):
             main = got[:, 128 * k : 128 * (k + 1)].reshape(8, SLOTS, 128)
             served_ref[pl.ds(at, 8), :, 128 * k : 128 * (k + 1)] = jnp.where(place == SLOTS - 1, part, main)
         to = spot_minus(m)
 
         def start(i, j):
-            dom_copy(served_ref.at[i], fetched_ref.at[i], serve_send, serve_recv.at[m], z_minus[j] + to).start()
+            dom_copy(served_ref.at[i, high], fetched_ref.at[i, high], serve_send, high_recv, z_minus[j] + to).start()
 
         for j in range(7):
             start(m * 8 + j, j)
@@ -208,7 +210,14 @@
         def _():
             start(m * 8 + 7, 7)
 
-    pltpu.make_async_copy(served_ref.at[others], fetched_ref.at[others], serve_recv.at[7]).start()
+    pltpu.make_async_copy(served_ref.at[others, high], fetched_ref.at[others, high], high_recv).start()
+
+    def start_low(i, m, j):
+        dom_copy(
+            served_ref.at[i, low], fetched_ref.at[i, low], serve_send, serve_recv.at[m], z_minus[j] + spot_minus(m)).start()
+
+    to_all(start_low, lambda: pltpu.make_async_copy(
+        served_ref.at[others, low], fetched_ref.at[others, low], serve_recv.at[7]).start())
 
     hot = onehot(iota((edges, rows), 1) == column(head_row))
     oh_ref[slots:, :] = hot
@@ -223,17 +232,7 @@
 
     slot_col = column(slot)
     fold = fold_matrix(256, 128)
-    got_ref[...] = jnp.zeros_like(got_ref)
-
-    @pl.loop(0, 4)
-    def _(b):
-        at = pl.ds(pl.multiple_of(b * 16, 16), 16)
-        for k in range(2):
-            half = pl.ds(pl.multiple_of(b * 16, 16) + 8 * k, 8)
-            pltpu.make_async_copy(served_ref.at[half], fetched_ref.at[half], serve_recv.at[2 * b + k]).wait()
-        hot = onehot(iota((lists, 16 * SLOTS), 1) + b * (16 * SLOTS) == slot_col)
-        got_ref[:, 0:MAIN] += dot_parts(hot, parts(fetched_ref[at].reshape(16 * SLOTS, MAIN), 3))
-
+    pltpu.make_async_copy(served_ref.at[:, high], fetched_ref.at[:, high], high_recv).wait()
     packed = parts(fetched_ref[:, SLOTS - 1, 0:256], 3)
 
     def remainders(at):
@@ -244,7 +243,9 @@
         return sum(dot(p, fold, NN) for p in parts(rest, 3))
 
     own = slice(edges, edges + quarter)
-    negs_ref[g, :, 0:MAIN] = got_ref[own, 0:MAIN]
+    line = iota((quarter, peers * 8), 1)
+    hot = onehot((line >> 3) * SLOTS + 8 + (line & 7) == slot_col[own])
+    negs_ref[g, :, 0:MAIN] = dot_parts(hot, parts(fetched_ref[:, 8:SLOTS, :].reshape(peers * 8, MAIN), 3))
     negs_ref[g, :, MAIN:WIDE] = remainders(own)
 
     def rel_copy(src, dst, send, recv, k):
@@ -254,8 +255,20 @@
     copies = [rel_copy(negs_ref.at[g], negs_ref.at[g], neg_send.at[k - 1], neg_recv.at[k - 1], k) for k in range(1, n)]
     for copy in copies:
         copy.start()
-    got_ref[0:edges, MAIN:WIDE] = remainders(slice(0, edges))
-    positive = jnp.sum(query_ref[...] * got_ref[0:edges, :], axis=1, keepdims=True)
+    tails = slice(0, edges)
+    got_ref[:, 0:MAIN] = jnp.zeros((edges, MAIN), F32)
+    got_ref[:, MAIN:WIDE] = remainders(tails)
+
+    @pl.loop(0, 4)
+    def _(b):
+        at = pl.ds(pl.multiple_of(b * 16, 16), 16)
+        for k in range(2):
+            part = pl.ds(pl.multiple_of(b * 16, 16) + 8 * k, 8)
+            pltpu.make_async_copy(served_ref.at[part, low], fetched_ref.at[part, low], serve_recv.at[2 * b + k]).wait()
+        hot = onehot(iota((edges, 16 * SLOTS), 1) + b * (16 * SLOTS) == slot_col[tails])
+        got_ref[:, 0:MAIN] += dot_parts(hot, parts(fetched_ref[at].reshape(16 * SLOTS, MAIN), 3))
+
+    positive = jnp.sum(query_ref[...] * got_ref[...], axis=1, keepdims=True)
     for copy in copies:
         copy.wait_recv()
     sent = list(copies)
@@ -284,11 +297,21 @@
             gn_ref[q, inside : inside + count] = grad_neg[first - c * SPAN : first - c * SPAN + count]
             first += count
 
-    copies = [
-        rel_copy(gn_ref.at[lax.rem(g + k, n)], gn_held.at[k - 1], gn_send.at[k - 1], gn_recv.at[k - 1], k) for k in range(1, n)
-    ]
-    for copy in copies:
+    right_hand, left_hand, far = lax.rem(g + 1, n), lax.rem(g + 3, n), lax.rem(g + 2, n)
+    to_of, back_of = (right_hand, left_hand), (left_hand, right_hand)
+    top, bottom = slice(0, quarter // 2), slice(quarter // 2, quarter)
+    two_hops, one_hop = (top, bottom), (bottom, top)
+
+    def gn_copy(way, step, src):
+        copy = pltpu.make_async_remote_copy(
+            src, gn_held.at[way, step], gn_send.at[way, step], gn_recv.at[way, step],
+            device_id={"rel": to_of[way]}, device_id_type=MESH)
         copy.start()
+        sent.append(copy)
+        return copy
+
+    firsts = [gn_copy(way, 0, gn_ref.at[far, two_hops[way]]) for way in range(2)]
+    arrivals = [gn_copy(way, 1, gn_ref.at[to_of[way], one_hop[way]]) for way in range(2)]
 
     def send_back(k, part, at):
         def start(i, m, j):
@@ -301,11 +324,14 @@
         to_all(start, own)
 
     hot = onehot(iota((slots, edges), 0) == slot[:, 0:edges])
-    low, high, all_rows = pl.ds(0, 8), pl.ds(8, 8), pl.ds(0, SLOTS)
     for k in range(CHUNKS):
         back_ref[k] = dot_parts(hot, parts(gt_ref[:, 128 * k : 128 * (k + 1)], 2)).reshape(peers, SLOTS, 128)
         if k == 0:
             send_back(0, 0, low)
+            for way in range(2):
+                firsts[way].wait_recv()
+                gn_sums[way] = gn_ref[to_of[way], two_hops[way]] + gn_held[way, 0]
+                arrivals.append(gn_copy(way, 2, gn_sums.at[way]))
 
     spread = spread_matrix(128, 256)
 
@@ -316,10 +342,10 @@
         return dot_parts(onehot(iota((peers, count), 0) == (slot[:, at] >> 4)), parts(rest, 2))
 
     rest = remainders_back(gt_ref[:, MAIN:WIDE], slice(0, edges))
-    for copy in copies:
+    for copy in arrivals:
         copy.wait_recv()
-    sent += copies
-    grad_neg = gn_ref[g] + gn_held[0] + gn_held[1] + gn_held[2]
+    grad_neg = jnp.concatenate(
+        [gn_ref[g, two_hops[way]] + gn_held[way, 2] + gn_held[1 - way, 1] for way in range(2)], axis=0)
     rest = rest + remainders_back(grad_neg[:, MAIN:WIDE], own)
     line = iota((peers * 8, quarter), 0)
     hot = onehot((line >> 3) * SLOTS + 8 + (line & 7) == slot[:, own])
@@ -351,7 +377,6 @@
 
     slab_ref = et_ref
     piece = rows // n
-    right_hand, left_hand, far = lax.rem(g + 1, n), lax.rem(g + 3, n), lax.rem(g + 2, n)
     first_row = [128 * k for k in range(CHUNKS)]
     height = [128] * (CHUNKS - 1) + [width - 128 * (CHUNKS - 1)]
 
@@ -359,7 +384,6 @@
         return pl.ds(pl.multiple_of(j * piece, piece), piece)
 
     ring = {}
-    to_of, back_of = (right_hand, left_hand), (left_hand, right_hand)
 
     def half(k, way, mine):
         h = height[k] // 2
@@ -485,35 +509,35 @@
     lists = WIDE
     slots = peers * SLOTS
     tall = (width - 128 * (CHUNKS - 1)) // 2
-    lists_of = [a.reshape(1, a.shape[0]) for a in (tail_owner, tail_row, head_row, rel_id, neg_owner, neg_row)]
-    ends = [sum(a.shape[1] for a in lists_of[: k + 1]) for k in range(len(lists_of))]
-    joined = sum(
-        jnp.pad(a, ((0, 0), (end - a.shape[1], ends[-1] - end))) for a, end in zip(lists_of, ends, strict=True))
+    lists_of = (tail_row, head_row, rel_id, neg_row)
+    ends = [sum(a.shape[0] for a in lists_of[: k + 1]) for k in range(len(lists_of))]
+    joined = sum(jnp.pad(a, (end - a.shape[0], ends[-1] - end)) for a, end in zip(lists_of, ends, strict=True))
+    joined = joined.reshape(1, ends[-1])
     V, DMA = pltpu.VMEM, pltpu.SemaphoreType.DMA
     vmem, in_hbm = pl.BlockSpec(memory_space=pltpu.VMEM), pl.BlockSpec(memory_space=pltpu.HBM)
     scratch = [
         V((groups, width), F32), V((width, rows), F32), V((WIDE, rows), BF16), V((WIDE, rows), BF16), V((WIDE, rows), BF16),
         V((slots + edges, rows), BF16), V((8, 1, 128), I32), V((8, 1, 128), I32), V((peers, 1, 128), I32),
-        V((peers, SLOTS, MAIN), F32), V((peers, SLOTS, MAIN), F32), V((lists, WIDE), F32), V((n, quarter, WIDE), F32),
+        V((peers, SLOTS, MAIN), F32), V((peers, SLOTS, MAIN), F32), V((edges, WIDE), F32), V((n, quarter, WIDE), F32),
         V((edges, WIDE), F32), V((edges, WIDE), F32), V((edges, WIDE), F32), V((edges, WIDE), F32), V((edges, WIDE), F32),
-        V((n, quarter, WIDE), F32), V((n - 1, quarter, WIDE), F32),
+        V((n, quarter, WIDE), F32), V((2, 3, quarter // 2, WIDE), F32), V((2, quarter // 2, WIDE), F32),
         V((CHUNKS, peers, SLOTS, 128), F32), V((CHUNKS, peers, SLOTS, 128), F32),
         V((2 * tall, slots + edges), BF16), V((2 * tall, slots + edges), BF16),
         V((CHUNKS, 2, 3, tall, rows // n), F32), V((CHUNKS, 2, tall, rows // n), F32),
         V((groups, 1, WIDE), F32), V((peers, 1, WIDE), F32), V((1, 1, WIDE), F32), V((groups, 1, WIDE), F32),
-        DMA((2,)), DMA(()), DMA(()), DMA(()), DMA(()), DMA(()), DMA((8,)), DMA((n - 1,)), DMA((n - 1,)), DMA((n - 1,)), DMA((n - 1,)),
+        DMA((2,)), DMA(()), DMA(()), DMA(()), DMA(()), DMA(()), DMA(()), DMA((8,)), DMA((n - 1,)), DMA((n - 1,)), DMA((2, 3)), DMA((2, 3)),
         DMA(()), DMA((CHUNKS + 1,)), DMA(()), DMA(()), DMA(()), DMA(()), DMA((CHUNKS, 2, 6)), DMA((CHUNKS, 2, 6)),
     ]
     total, relation = pl.pallas_call(
         kernel,
         out_shape=(jax.ShapeDtypeStruct((width, rows), F32), jax.ShapeDtypeStruct((groups, width), F32)),
-        in_specs=[vmem, in_hbm, in_hbm],
+        in_specs=[vmem, vmem, vmem, in_hbm, in_hbm],
         out_specs=(vmem, vmem),
         scratch_shapes=scratch,
         compiler_params=pltpu.CompilerParams(collective_id=0, has_side_effects=True, vmem_limit_bytes=48 << 20),
         cost_estimate=pl.CostEstimate(flops=int(3e10), bytes_accessed=7 << 20, transcendentals=0),
         name="ranking_gradients",
-    )(joined, rel_weight, embeddings.T)
+    )(joined, tail_owner.reshape(1, edges), neg_owner.reshape(1, negs), rel_weight, embeddings.T)
     return (total.T, relation)
 
 

time: 158 us -> 148 us (0.937)
  Pallas kernels: 151 us -> 141 us
    pallas_call x1, Pallas kernels: 151 us -> 141 us  [body(): pl.pallas_call(kernel, out_shape=(jax.ShapeDtypeStruct((width, rows), F32...]
    reshape x4 -> x1, local copies, waits for them, and re-layouts: 2.73 us -> 0.01 us  [body(): joined = joined.reshape(1, ends[-1])]
    unnamed x4 -> x8, local copies, waits for them, and re-layouts: 3.27 us -> 4.62 us
where the time goes in v5:
time: 148 us; the launch traced here: 147 us
  Pallas kernels  141 us (95%)
  local copies, waits for them, and re-layouts  4.63 us (3%)
    pallas_call x1, Pallas kernels, body(): pl.pallas_call(kernel, out_shape=(jax.ShapeDtypeStruct((width, rows), F32...  141 us
    unnamed x8, local copies, waits for them, and re-layouts  4.62 us

profile of v5, /device:TPU:2, one launch (start us, length us, event | category | flops | bytes accessed | tf_op | source)
XLA Modules:
  0.0 146.9 jit_solution(8602327306540861729)
XLA Ops:
  0.6 0.7 pad_add_fusion
  1.4 0.0 copy-start
  1.4 0.9 copy-done
  2.3 0.0 copy-start.1
  2.3 0.7 copy-done.1
  3.0 0.0 copy-start.2
  3.0 0.7 copy-done.2
  3.6 140.8 %ranking_gradients.1 = (f32[400,2048]{1,0:T(8,128)S(1)}, f32[64,400]{1,0:T(8,128)S(1)}) custom-call(s32[1,1536]{1,0:T(1,128)S(1)} %reshape.13.lists_ref, s32[1,384]{1,0:T(1,128)S(1)} %bitcast.5, s32[1,384]{1,0:T(1,128)S(1)} %bitcast.6, f32[64,400]{1,0:T(8,128)S(1)} %copy-done, f32[400,2048]{1,0:T(8,128)} %bitcast.7), custom_call_target="tpu_custom_call" | custom-call | flops 30000001024 | bytes 7340032 | tf_op jit(solution)/shard_map/ranking_gradients/pallas_call | solution.py:531
  144.5 1.7 %copy.12 = f32[2048,400]{0,1:T(8,128)} copy(f32[2048,400]{0,1:T(8,128)S(1)} %bitcast.4) | data formatting | bytes 6553600
  146.2 0.7 copy.13
  (1 shorter events, 0.0 us)
Async XLA Ops:
  1.4 0.9 copy-start
  2.3 0.7 copy-start.1
  3.0 0.7 copy-start.2

commit v6 on v5

--- a/solution.py
+++ b/solution.py
@@ -76,7 +76,7 @@
     lists_ref, towner_ref, nowner_ref, rel_in, et_in,
     out_ref, rel_out,
     rel_ref, et_ref, hi_ref, mid_ref, lo_ref, oh_ref, ids_ref, line_ref, asked_ref, served_ref, fetched_ref, got_ref, negs_ref,
-    head_emb, rel_rows, query_ref, gh_ref, gt_ref, gn_ref, gn_held, gn_sums, back_ref, recv_ref, vt_hi, vt_lo, held_ref, sums_ref,
+    head_emb, rel_rows, query_ref, gh_ref, gt_ref, gn_ref, gn_held, gn_sums, back_ref, recv_ref, vt_ref, held_ref, sums_ref,
     gr_ref, gr_recv, gr_sum, rel_recv,
     load_sem, ids_send, ids_recv, line_send, line_recv, serve_send, high_recv, serve_recv, neg_send, neg_recv, gn_send, gn_recv,
     back_send, back_recv, gr_send, gr_got, ag_send, ag_recv, ring_send, ring_recv,
@@ -134,8 +134,8 @@
     for k in range(1, n):
         pl.semaphore_signal(barrier, inc=1, device_id={"rel": lax.rem(g + k, n)}, device_id_type=MESH)
 
-    tail_row, head_row, rel_id = (lists_ref[:, edges * k : edges * (k + 1)] for k in range(3))
-    neg_row = lists_ref[:, 3 * edges : 3 * edges + negs]
+    tail_row, head_row, rel_id = (lists_ref[edges * k : edges * (k + 1)][None, :] for k in range(3))
+    neg_row = lists_ref[3 * edges : 3 * edges + negs][None, :]
 
     def mine(row):
         return sum(jnp.where(g == q, row[:, quarter * q : quarter * (q + 1)], 0) for q in range(n))
@@ -162,20 +162,23 @@
     for j in range(7):
         dom_copy(ids_ref.at[j], line_ref.at[j], ids_send, ids_recv, z_plus[j] + spot).start()
     pltpu.make_async_copy(ids_ref.at[7], line_ref.at[7], ids_recv).start()
+    for load in loads:
+        load.wait()
+
+    def split(start, stop):
+        @pl.loop(start, stop)
+        def _(i):
+            at = pl.multiple_of(i * 16, 16)
+            for t, v in zip(tables, parts(et_ref[pl.ds(at, 16), :], 3), strict=True):
+                t[pl.ds(at, 16), :] = v
+
+    split(0, width // 32)
     pltpu.make_async_copy(ids_ref, line_ref, ids_recv).wait()
     for m in range(7):
         dom_copy(line_ref, asked_ref.at[8 * m : 8 * m + 8], line_send, line_recv, z * 8 + spot_plus(m)).start()
     pltpu.make_async_copy(line_ref, asked_ref.at[56:64], line_recv).start()
 
-    for load in loads:
-        load.wait()
-
-    @pl.loop(0, width // 16)
-    def _(i):
-        at = pl.multiple_of(i * 16, 16)
-        for t, v in zip(tables, parts(et_ref[pl.ds(at, 16), :], 3), strict=True):
-            t[pl.ds(at, 16), :] = v
-
+    split(width // 32, width // 16)
     for t in tables:
         for k in range(1, 8):
             t[MAIN + 16 * k : MAIN + 16 * (k + 1), :] = t[MAIN : MAIN + 16, :]
@@ -302,16 +305,36 @@
     top, bottom = slice(0, quarter // 2), slice(quarter // 2, quarter)
     two_hops, one_hop = (top, bottom), (bottom, top)
 
-    def gn_copy(way, step, src):
+    part_cols = (slice(0, 128), slice(128, WIDE))
+
+    def gn_copy(part, way, step, src):
         copy = pltpu.make_async_remote_copy(
-            src, gn_held.at[way, step], gn_send.at[way, step], gn_recv.at[way, step],
+            src, gn_held.at[way, step, :, part_cols[part]], gn_send.at[part, way, step], gn_recv.at[part, way, step],
             device_id={"rel": to_of[way]}, device_id_type=MESH)
         copy.start()
         sent.append(copy)
         return copy
 
-    firsts = [gn_copy(way, 0, gn_ref.at[far, two_hops[way]]) for way in range(2)]
-    arrivals = [gn_copy(way, 1, gn_ref.at[to_of[way], one_hop[way]]) for way in range(2)]
+    def gn_begin(part):
+        at = part_cols[part]
+        two = [gn_copy(part, way, 0, gn_ref.at[far, two_hops[way], at]) for way in range(2)]
+        return two, [gn_copy(part, way, 1, gn_ref.at[to_of[way], one_hop[way], at]) for way in range(2)]
+
+    def gn_add(part, begun):
+        at = part_cols[part]
+        for way in range(2):
+            begun[0][way].wait_recv()
+            gn_sums[way, :, at] = gn_ref[to_of[way], two_hops[way], at] + gn_held[way, 0, :, at]
+            begun[1].append(gn_copy(part, way, 2, gn_sums.at[way, :, at]))
+
+    def gn_total(part, begun):
+        at = part_cols[part]
+        for copy in begun[1]:
+            copy.wait_recv()
+        return jnp.concatenate(
+            [gn_ref[g, two_hops[way], at] + gn_held[way, 2, :, at] + gn_held[1 - way, 1, :, at] for way in range(2)], axis=0)
+
+    begun = [gn_begin(0)]
 
     def send_back(k, part, at):
         def start(i, m, j):
@@ -323,15 +346,15 @@
 
         to_all(start, own)
 
-    hot = onehot(iota((slots, edges), 0) == slot[:, 0:edges])
-    for k in range(CHUNKS):
-        back_ref[k] = dot_parts(hot, parts(gt_ref[:, 128 * k : 128 * (k + 1)], 2)).reshape(peers, SLOTS, 128)
-        if k == 0:
-            send_back(0, 0, low)
-            for way in range(2):
-                firsts[way].wait_recv()
-                gn_sums[way] = gn_ref[to_of[way], two_hops[way]] + gn_held[way, 0]
-                arrivals.append(gn_copy(way, 2, gn_sums.at[way]))
+    tail_hot = onehot(iota((slots, edges), 0) == slot[:, 0:edges])
+
+    def pack_tails(k):
+        back_ref[k] = dot_parts(tail_hot, parts(gt_ref[:, 128 * k : 128 * (k + 1)], 2)).reshape(peers, SLOTS, 128)
+
+    pack_tails(0)
+    gn_add(0, begun[0])
+    begun.append(gn_begin(1))
+    send_back(0, 0, low)
 
     spread = spread_matrix(128, 256)
 
@@ -342,21 +365,24 @@
         return dot_parts(onehot(iota((peers, count), 0) == (slot[:, at] >> 4)), parts(rest, 2))
 
     rest = remainders_back(gt_ref[:, MAIN:WIDE], slice(0, edges))
-    for copy in arrivals:
-        copy.wait_recv()
-    grad_neg = jnp.concatenate(
-        [gn_ref[g, two_hops[way]] + gn_held[way, 2] + gn_held[1 - way, 1] for way in range(2)], axis=0)
-    rest = rest + remainders_back(grad_neg[:, MAIN:WIDE], own)
     line = iota((peers * 8, quarter), 0)
-    hot = onehot((line >> 3) * SLOTS + 8 + (line & 7) == slot[:, own])
+    neg_hot = onehot((line >> 3) * SLOTS + 8 + (line & 7) == slot[:, own])
     last = iota((peers, 8, 128), 1) == 7
-    for k in range(CHUNKS):
-        more = dot_parts(hot, parts(grad_neg[:, 128 * k : 128 * (k + 1)], 2)).reshape(peers, 8, 128)
+
+    def pack_rest(k, grad_neg, rest):
+        more = dot_parts(neg_hot, parts(grad_neg, 2)).reshape(peers, 8, 128)
         more = back_ref[k, :, 8:SLOTS, :] + more
         if k < 2:
             more = jnp.where(last, rest[:, 128 * k : 128 * (k + 1)][:, None, :], more)
         back_ref[k, :, 8:SLOTS, :] = more
         send_back(k, k + 1, high if k == 0 else all_rows)
+
+    pack_rest(0, gn_total(0, begun[0]), rest)
+    gn_add(1, begun[1])
+    pack_tails(1)
+    grad_neg = gn_total(1, begun[1])
+    rest = rest + remainders_back(grad_neg[:, MAIN - 128 :], own)
+    pack_rest(1, grad_neg[:, 0:128], rest)
 
     gr_parts = []
     for c in range(edges // SPAN):
@@ -368,12 +394,6 @@
         hot = onehot(iota((groups, SPAN), 0) == rel_id[:, at])
         gr_parts.append(dot_parts(hot, parts(grad_query * head_emb[at], 3)))
     gr_ref[...] = sum(gr_parts)[:, None, :]
-
-    def start_rel(i, m, j):
-        to = z_plus[j] + spot_plus(m)
-        dom_copy(gr_ref.at[to], gr_recv.at[i], gr_send, gr_got, to).start()
-
-    to_all(start_rel, lambda: pltpu.make_async_copy(gr_ref.at[me], gr_recv.at[others], gr_got).start())
 
     slab_ref = et_ref
     piece = rows // n
@@ -417,13 +437,13 @@
             more = jnp.concatenate([rest.T[0:16], gh_ref[:, MAIN:WIDE].T[0:16]], axis=1)
             vt = jnp.concatenate([vt, more], axis=0)
         h = height[k]
-        vt_hi[0:h], vt_lo[0:h] = parts(vt, 2)
+        vt_ref[0:h], vt_ref[h : 2 * h] = parts(vt, 2)
 
         @pl.loop(0, n)
         def _(j):
             at = cols(j)
-            slab_ref[first_row[k] : first_row[k] + h, at] = dot(vt_hi[0:h], oh_ref[:, at], NN) + dot(
-                vt_lo[0:h], oh_ref[:, at], NN)
+            both = dot(vt_ref[0 : 2 * h], oh_ref[:, at], NN)
+            slab_ref[first_row[k] : first_row[k] + h, at] = both[0:h] + both[h : 2 * h]
 
     def begin(k):
         h = height[k] // 2
@@ -460,10 +480,18 @@
 
     scatter(0)
     begin(0)
+    pack_tails(2)
+    pack_rest(2, grad_neg[:, 128:256], rest)
     add(0)
     share(0)
     scatter(1)
     begin(1)
+
+    def start_rel(i, m, j):
+        to = z_plus[j] + spot_plus(m)
+        dom_copy(gr_ref.at[to], gr_recv.at[i], gr_send, gr_got, to).start()
+
+    to_all(start_rel, lambda: pltpu.make_async_copy(gr_ref.at[me], gr_recv.at[others], gr_got).start())
     forward(0)
     add(1)
     share(1)
@@ -512,7 +540,6 @@
     lists_of = (tail_row, head_row, rel_id, neg_row)
     ends = [sum(a.shape[0] for a in lists_of[: k + 1]) for k in range(len(lists_of))]
     joined = sum(jnp.pad(a, (end - a.shape[0], ends[-1] - end)) for a, end in zip(lists_of, ends, strict=True))
-    joined = joined.reshape(1, ends[-1])
     V, DMA = pltpu.VMEM, pltpu.SemaphoreType.DMA
     vmem, in_hbm = pl.BlockSpec(memory_space=pltpu.VMEM), pl.BlockSpec(memory_space=pltpu.HBM)
     scratch = [
@@ -522,10 +549,10 @@
         V((edges, WIDE), F32), V((edges, WIDE), F32), V((edges, WIDE), F32), V((edges, WIDE), F32), V((edges, WIDE), F32),
         V((n, quarter, WIDE), F32), V((2, 3, quarter // 2, WIDE), F32), V((2, quarter // 2, WIDE), F32),
         V((CHUNKS, peers, SLOTS, 128), F32), V((CHUNKS, peers, SLOTS, 128), F32),
-        V((2 * tall, slots + edges), BF16), V((2 * tall, slots + edges), BF16),
+        V((4 * tall, slots + edges), BF16),
         V((CHUNKS, 2, 3, tall, rows // n), F32), V((CHUNKS, 2, tall, rows // n), F32),
         V((groups, 1, WIDE), F32), V((peers, 1, WIDE), F32), V((1, 1, WIDE), F32), V((groups, 1, WIDE), F32),
-        DMA((2,)), DMA(()), DMA(()), DMA(()), DMA(()), DMA(()), DMA(()), DMA((8,)), DMA((n - 1,)), DMA((n - 1,)), DMA((2, 3)), DMA((2, 3)),
+        DMA((2,)), DMA(()), DMA(()), DMA(()), DMA(()), DMA(()), DMA(()), DMA((8,)), DMA((n - 1,)), DMA((n - 1,)), DMA((2, 2, 3)), DMA((2, 2, 3)),
         DMA(()), DMA((CHUNKS + 1,)), DMA(()), DMA(()), DMA(()), DMA(()), DMA((CHUNKS, 2, 6)), DMA((CHUNKS, 2, 6)),
     ]
     total, relation = pl.pallas_call(

time: 148 us -> 146 us (0.986)
  no operation moved by 1% of the time
where the time goes in v6:
time: 146 us
  Pallas kernels  140 us (96%)
  local copies, waits for them, and re-layouts  4.63 us (3%)
    pallas_call x1, Pallas kernels, body(): pl.pallas_call(kernel, out_shape=(jax.ShapeDtypeStruct((width, rows), F32...  140 us
    unnamed x8, local copies, waits for them, and re-layouts  4.63 us

profile of v6, /device:TPU:2, one launch (start us, length us, event | category | flops | bytes accessed | tf_op | source)
XLA Modules:
  0.0 145.6 jit_solution(9898094626217171183)
XLA Ops:
  0.6 0.7 pad_add_fusion.lists_ref
  1.4 0.0 copy-start
  1.4 0.9 copy-done
  2.3 0.0 copy-start.1
  2.3 0.7 copy-done.1
  3.0 0.0 copy-start.2
  3.0 0.7 copy-done.2
  3.6 139.6 %ranking_gradients.1 = (f32[400,2048]{1,0:T(8,128)S(1)}, f32[64,400]{1,0:T(8,128)S(1)}) custom-call(s32[1536]{0:T(1024)S(1)} %pad_add_fusion.lists_ref, s32[1,384]{1,0:T(1,128)S(1)} %bitcast.5, s32[1,384]{1,0:T(1,128)S(1)} %bitcast.6, f32[64,400]{1,0:T(8,128)S(1)} %copy-done, f32[400,2048]{1,0:T(8,128)} %bitcast.7), custom_call_target="tpu_custom_call" | custom-call | flops 30000001024 | bytes 7340032 | tf_op jit(solution)/shard_map/ranking_gradients/pallas_call | solution.py:558
  143.3 1.7 %copy.12 = f32[2048,400]{0,1:T(8,128)} copy(f32[2048,400]{0,1:T(8,128)S(1)} %bitcast.4) | data formatting | bytes 6553600
  145.0 0.7 copy.13
Async XLA Ops:
  1.4 0.9 copy-start
  2.3 0.7 copy-start.1
  3.0 0.7 copy-start.2

commit v7 on v6

--- a/solution.py
+++ b/solution.py
@@ -77,7 +77,7 @@
     out_ref, rel_out,
     rel_ref, et_ref, hi_ref, mid_ref, lo_ref, oh_ref, ids_ref, line_ref, asked_ref, served_ref, fetched_ref, got_ref, negs_ref,
     head_emb, rel_rows, query_ref, gh_ref, gt_ref, gn_ref, gn_held, gn_sums, back_ref, recv_ref, vt_ref, held_ref, sums_ref,
-    gr_ref, gr_recv, gr_sum, rel_recv,
+    gr_ref, gr_recv, gr_sum, rel_recv, score_ref, tail_hot, neg_hot,
     load_sem, ids_send, ids_recv, line_send, line_recv, serve_send, high_recv, serve_recv, neg_send, neg_recv, gn_send, gn_recv,
     back_send, back_recv, gr_send, gr_got, ag_send, ag_recv, ring_send, ring_recv,
 ):
@@ -262,8 +262,7 @@
     got_ref[:, 0:MAIN] = jnp.zeros((edges, MAIN), F32)
     got_ref[:, MAIN:WIDE] = remainders(tails)
 
-    @pl.loop(0, 4)
-    def _(b):
+    def unpack(b):
         at = pl.ds(pl.multiple_of(b * 16, 16), 16)
         for k in range(2):
             part = pl.ds(pl.multiple_of(b * 16, 16) + 8 * k, 8)
@@ -271,7 +270,8 @@
         hot = onehot(iota((edges, 16 * SLOTS), 1) + b * (16 * SLOTS) == slot_col[tails])
         got_ref[:, 0:MAIN] += dot_parts(hot, parts(fetched_ref[at].reshape(16 * SLOTS, MAIN), 3))
 
-    positive = jnp.sum(query_ref[...] * got_ref[...], axis=1, keepdims=True)
+    pl.loop(0, 3)(unpack)
+
     for copy in copies:
         copy.wait_recv()
     sent = list(copies)
@@ -279,20 +279,26 @@
     def neg_rows(c):
         return negs_ref[...].reshape(negs, WIDE)[c * SPAN : (c + 1) * SPAN]
 
-    coefs = []
     for c in range(edges // SPAN):
         at = slice(c * SPAN, (c + 1) * SPAN)
-        queries = query_ref[at]
-        scores = lax.dot_general(queries, neg_rows(c), NT, precision=HIGHEST, preferred_element_type=F32)
-        row_max = jnp.maximum(positive[at], jnp.max(scores, axis=1, keepdims=True))
-        pos_exp = jnp.exp(positive[at] - row_max)
-        neg_exp = jnp.exp(scores - row_max)
-        total = pos_exp + jnp.sum(neg_exp, axis=1, keepdims=True)
-        pos_coef = pos_exp / total - 1.0
-        neg_coef = neg_exp / total
-        coefs.append((pos_coef, neg_coef))
-        gt_ref[at] = pos_coef * queries
-        grad_neg = lax.dot_general(neg_coef.T, queries, NN, precision=HIGHEST, preferred_element_type=F32)
+        score_ref[at] = lax.dot_general(query_ref[at], neg_rows(c), NT, precision=HIGHEST, preferred_element_type=F32)
+    tail_hot[...] = onehot(iota((slots, edges), 0) == slot[:, 0:edges])
+    line = iota((peers * 8, quarter), 0)
+    neg_hot[...] = onehot((line >> 3) * SLOTS + 8 + (line & 7) == slot[:, own])
+    unpack(3)
+
+    positive = jnp.sum(query_ref[...] * got_ref[...], axis=1, keepdims=True)
+    scores = score_ref[...]
+    row_max = jnp.maximum(positive, jnp.max(scores, axis=1, keepdims=True))
+    pos_exp = jnp.exp(positive - row_max)
+    neg_exp = jnp.exp(scores - row_max)
+    total = pos_exp + jnp.sum(neg_exp, axis=1, keepdims=True)
+    pos_coef = pos_exp / total - 1.0
+    neg_coef = neg_exp / total
+    gt_ref[...] = pos_coef * query_ref[...]
+    for c in range(edges // SPAN):
+        at = slice(c * SPAN, (c + 1) * SPAN)
+        grad_neg = lax.dot_general(neg_coef[at].T, query_ref[at], NN, precision=HIGHEST, preferred_element_type=F32)
         first = c * SPAN
         while first < (c + 1) * SPAN:
             q, inside = divmod(first, quarter)
@@ -346,15 +352,13 @@
 
         to_all(start, own)
 
-    tail_hot = onehot(iota((slots, edges), 0) == slot[:, 0:edges])
-
     def pack_tails(k):
-        back_ref[k] = dot_parts(tail_hot, parts(gt_ref[:, 128 * k : 128 * (k + 1)], 2)).reshape(peers, SLOTS, 128)
+        back_ref[k] = dot_parts(tail_hot[...], parts(gt_ref[:, 128 * k : 128 * (k + 1)], 2)).reshape(peers, SLOTS, 128)
 
     pack_tails(0)
+    send_back(0, 0, low)
     gn_add(0, begun[0])
     begun.append(gn_begin(1))
-    send_back(0, 0, low)
 
     spread = spread_matrix(128, 256)
 
@@ -365,12 +369,10 @@
         return dot_parts(onehot(iota((peers, count), 0) == (slot[:, at] >> 4)), parts(rest, 2))
 
     rest = remainders_back(gt_ref[:, MAIN:WIDE], slice(0, edges))
-    line = iota((peers * 8, quarter), 0)
-    neg_hot = onehot((line >> 3) * SLOTS + 8 + (line & 7) == slot[:, own])
     last = iota((peers, 8, 128), 1) == 7
 
     def pack_rest(k, grad_neg, rest):
-        more = dot_parts(neg_hot, parts(grad_neg, 2)).reshape(peers, 8, 128)
+        more = dot_parts(neg_hot[...], parts(grad_neg, 2)).reshape(peers, 8, 128)
         more = back_ref[k, :, 8:SLOTS, :] + more
         if k < 2:
             more = jnp.where(last, rest[:, 128 * k : 128 * (k + 1)][:, None, :], more)
@@ -387,9 +389,8 @@
     gr_parts = []
     for c in range(edges // SPAN):
         at = slice(c * SPAN, (c + 1) * SPAN)
-        pos_coef, neg_coef = coefs[c]
-        grad_query = pos_coef * got_ref[at] + lax.dot_general(
-            neg_coef, neg_rows(c), NN, precision=HIGHEST, preferred_element_type=F32)
+        grad_query = pos_coef[at] * got_ref[at] + lax.dot_general(
+            neg_coef[at], neg_rows(c), NN, precision=HIGHEST, preferred_element_type=F32)
         gh_ref[at] = grad_query * rel_rows[at]
         hot = onehot(iota((groups, SPAN), 0) == rel_id[:, at])
         gr_parts.append(dot_parts(hot, parts(grad_query * head_emb[at], 3)))
@@ -552,6 +553,7 @@
         V((4 * tall, slots + edges), BF16),
         V((CHUNKS, 2, 3, tall, rows // n), F32), V((CHUNKS, 2, tall, rows // n), F32),
         V((groups, 1, WIDE), F32), V((peers, 1, WIDE), F32), V((1, 1, WIDE), F32), V((groups, 1, WIDE), F32),
+        V((edges, SPAN), F32), V((slots, edges), BF16), V((peers * 8, quarter), BF16),
         DMA((2,)), DMA(()), DMA(()), DMA(()), DMA(()), DMA(()), DMA(()), DMA((8,)), DMA((n - 1,)), DMA((n - 1,)), DMA((2, 2, 3)), DMA((2, 2, 3)),
         DMA(()), DMA((CHUNKS + 1,)), DMA(()), DMA(()), DMA(()), DMA(()), DMA((CHUNKS, 2, 6)), DMA((CHUNKS, 2, 6)),
     ]

time: 146 us -> 142 us (0.973)
  Pallas kernels: 140 us -> 136 us
    pallas_call x1, Pallas kernels: 140 us -> 136 us  [body(): pl.pallas_call(kernel, out_shape=(jax.ShapeDtypeStruct((width, rows), F32...]
where the time goes in v7:
time: 142 us
  Pallas kernels  136 us (96%)
  local copies, waits for them, and re-layouts  4.63 us (3%)
    pallas_call x1, Pallas kernels, body(): pl.pallas_call(kernel, out_shape=(jax.ShapeDtypeStruct((width, rows), F32...  136 us
    unnamed x8, local copies, waits for them, and re-layouts  4.63 us

profile of v7, /device:TPU:2, one launch (start us, length us, event | category | flops | bytes accessed | tf_op | source)
XLA Modules:
  0.0 142.2 jit_solution(10377725561616984511)
XLA Ops:
  0.6 0.7 pad_add_fusion.lists_ref
  1.4 0.0 copy-start
  1.4 0.9 copy-done
  2.3 0.0 copy-start.1
  2.3 0.7 copy-done.1
  3.0 0.0 copy-start.2
  3.0 0.7 copy-done.2
  3.6 136.2 %ranking_gradients.1 = (f32[400,2048]{1,0:T(8,128)S(1)}, f32[64,400]{1,0:T(8,128)S(1)}) custom-call(s32[1536]{0:T(1024)S(1)} %pad_add_fusion.lists_ref, s32[1,384]{1,0:T(1,128)S(1)} %bitcast.5, s32[1,384]{1,0:T(1,128)S(1)} %bitcast.6, f32[64,400]{1,0:T(8,128)S(1)} %copy-done, f32[400,2048]{1,0:T(8,128)} %bitcast.7), custom_call_target="tpu_custom_call" | custom-call | flops 30000001024 | bytes 7340032 | tf_op jit(solution)/shard_map/ranking_gradients/pallas_call | solution.py:560
  139.9 1.7 %copy.12 = f32[2048,400]{0,1:T(8,128)} copy(f32[2048,400]{0,1:T(8,128)S(1)} %bitcast.4) | data formatting | bytes 6553600
  141.6 0.7 copy.13
Async XLA Ops:
  1.4 0.9 copy-start
  2.3 0.7 copy-start.1
  3.0 0.7 copy-start.2

commit v8 on v7

--- a/solution.py
+++ b/solution.py
@@ -295,16 +295,18 @@
     total = pos_exp + jnp.sum(neg_exp, axis=1, keepdims=True)
     pos_coef = pos_exp / total - 1.0
     neg_coef = neg_exp / total
-    gt_ref[...] = pos_coef * query_ref[...]
-    for c in range(edges // SPAN):
-        at = slice(c * SPAN, (c + 1) * SPAN)
-        grad_neg = lax.dot_general(neg_coef[at].T, query_ref[at], NN, precision=HIGHEST, preferred_element_type=F32)
-        first = c * SPAN
-        while first < (c + 1) * SPAN:
-            q, inside = divmod(first, quarter)
-            count = min(quarter - inside, (c + 1) * SPAN - first)
-            gn_ref[q, inside : inside + count] = grad_neg[first - c * SPAN : first - c * SPAN + count]
-            first += count
+    turned = [neg_coef[c * SPAN : (c + 1) * SPAN].T for c in range(edges // SPAN)]
+
+    def neg_grads(at):
+        for c in range(edges // SPAN):
+            queries = query_ref[c * SPAN : (c + 1) * SPAN, at]
+            grad_neg = lax.dot_general(turned[c], queries, NN, precision=HIGHEST, preferred_element_type=F32)
+            first = c * SPAN
+            while first < (c + 1) * SPAN:
+                q, inside = divmod(first, quarter)
+                count = min(quarter - inside, (c + 1) * SPAN - first)
+                gn_ref[q, inside : inside + count, at] = grad_neg[first - c * SPAN : first - c * SPAN + count]
+                first += count
 
     right_hand, left_hand, far = lax.rem(g + 1, n), lax.rem(g + 3, n), lax.rem(g + 2, n)
     to_of, back_of = (right_hand, left_hand), (left_hand, right_hand)
@@ -340,7 +342,9 @@
         return jnp.concatenate(
             [gn_ref[g, two_hops[way], at] + gn_held[way, 2, :, at] + gn_held[1 - way, 1, :, at] for way in range(2)], axis=0)
 
+    neg_grads(part_cols[0])
     begun = [gn_begin(0)]
+    gt_ref[...] = pos_coef * query_ref[...]
 
     def send_back(k, part, at):
         def start(i, m, j):
@@ -357,6 +361,7 @@
 
     pack_tails(0)
     send_back(0, 0, low)
+    neg_grads(part_cols[1])
     gn_add(0, begun[0])
     begun.append(gn_begin(1))
 

time: 142 us -> 142 us (level)
  no operation moved by 1% of the time
where the time goes in v8:
time: 142 us; the launch traced here: 141 us
  Pallas kernels  135 us (95%)
  local copies, waits for them, and re-layouts  4.63 us (3%)
    pallas_call x1, Pallas kernels, body(): pl.pallas_call(kernel, out_shape=(jax.ShapeDtypeStruct((width, rows), F32...  135 us
    unnamed x8, local copies, waits for them, and re-layouts  4.63 us

profile of v8, /device:TPU:2, one launch (start us, length us, event | category | flops | bytes accessed | tf_op | source)
XLA Modules:
  0.0 141.2 jit_solution(2454195218533357773)
XLA Ops:
  0.6 0.7 pad_add_fusion.lists_ref
  1.4 0.0 copy-start
  1.4 0.9 copy-done
  2.3 0.0 copy-start.1
  2.3 0.7 copy-done.1
  3.0 0.0 copy-start.2
  3.0 0.7 copy-done.2
  3.6 135.1 %ranking_gradients.1 = (f32[400,2048]{1,0:T(8,128)S(1)}, f32[64,400]{1,0:T(8,128)S(1)}) custom-call(s32[1536]{0:T(1024)S(1)} %pad_add_fusion.lists_ref, s32[1,384]{1,0:T(1,128)S(1)} %bitcast.5, s32[1,384]{1,0:T(1,128)S(1)} %bitcast.6, f32[64,400]{1,0:T(8,128)S(1)} %copy-done, f32[400,2048]{1,0:T(8,128)} %bitcast.7), custom_call_target="tpu_custom_call" | custom-call | flops 30000001024 | bytes 7340032 | tf_op jit(solution)/shard_map/ranking_gradients/pallas_call | solution.py:565
  138.8 1.7 %copy.12 = f32[2048,400]{0,1:T(8,128)} copy(f32[2048,400]{0,1:T(8,128)S(1)} %bitcast.4) | data formatting | bytes 6553600
  140.5 0.7 copy.13
Async XLA Ops:
  1.4 0.9 copy-start
  2.3 0.7 copy-start.1
  3.0 0.7 copy-start.2
